TPU v7x, 128 devices: a whole 4x4x4 slice. The times are simulated.
128 devices in a mesh: dp: 32 (over y, z, core), tensor: 4 (over x).
Axes of the slice: x: 4, y: 4, z: 4, core: 2. Of those that a mesh axis runs over, the one named last changes fastest.
Arguments:
- inputs: bfloat16 [16384, 4096], P(('dp', 'tensor')), may hold values from -60 to 60
- output_gradient: bfloat16 [16384, 4096], P('dp', 'tensor'), may hold values from -60 to 60
- frozen: bfloat16 [4096, 4096], P('tensor'), may hold values from -0.09375 to 0.09375
- adapter_down_weight: bfloat16 [16, 4096], replicated, may hold values from -0.09375 to 0.09375
- adapter_up_weight: bfloat16 [16, 4096], P(None, 'tensor'), may hold values from -0.09375 to 0.09375
Outputs:
- input_gradient: bfloat16 [16384, 4096], P(('dp', 'tensor'))
- act_factor: float32 [4096, 4096], P('dp', 'tensor')
- grad_factor: float32 [4096, 4096], P('dp', 'tensor')
- grad_down: float32 [16, 4096], P(None, 'tensor')
- up_gradient_mean: float32 [16, 4096], P(None, 'tensor')
All inputs are finite; a program needn't handle non-finite values.
Results may differ from a plain program's by a relative error of at most 0.014.
Values may be sent and summed in bfloat16 or wider, within the bound.
No kernel may reach another device: no remote copies, remote signals or barrier semaphores. Data moves between devices by JAX's collectives and lax.ppermute only.
A program may use at most 256 MiB of HBM per device.

v0:
```python
import functools

import jax
import jax.numpy as jnp
from jax import lax
from jax.experimental import pallas as pl
from jax.experimental.pallas import tpu as pltpu
from jax.sharding import Mesh, PartitionSpec as P

adapter_scale = 2.0
f32 = jnp.float32
bf16 = jnp.bfloat16
ring = 4
lane = 128
vmem = 60 * 2**20
hbm = pl.BlockSpec(memory_space=pltpu.MemorySpace.HBM)
light = pl.CostEstimate(flops=2**10, bytes_accessed=2**10, transcendentals=0)


def shift(array, axis, step):
    size = lax.axis_size(axis)
    return lax.ppermute(array, axis, [(i, (i + step) % size) for i in range(size)])


def exchange(array, axis, step):
    return lax.ppermute(array, axis, [(i, i ^ step) for i in range(lax.axis_size(axis))])


def travel(array, axis, step):
    size = lax.axis_size(axis)
    sign = (1, -1)
    order = ("c", axis) if axis == "x" else (axis, "c")
    place = (lambda i, c: size * c + i) if axis == "x" else (lambda i, c: 2 * i + c)
    pairs = [(place(i, c), place((i + step * sign[c]) % size, c)) for i in range(size) for c in range(2)]
    return lax.ppermute(array, order, pairs)


def together(*values):
    return lax.optimization_barrier(values)


def cols(array, start, width):
    return lax.dynamic_slice_in_dim(array, start, width, 1)


def rows(array, start, width):
    return lax.dynamic_slice_in_dim(array, start, width, 0)


def nt(left, right):
    return lax.dot_general(left, right, (((1,), (1,)), ((), ())), preferred_element_type=f32)


def tn(left, right):
    return lax.dot_general(left, right, (((0,), (0,)), ((), ())), preferred_element_type=f32)


def mm(left, right):
    return jnp.dot(left, right, preferred_element_type=f32)


def run_all(copies):
    for copy in copies:
        copy.start()
    for copy in copies:
        copy.wait()


def share_kernel(left, right, out):
    out[...] = mm(left[...], right[...]).astype(bf16)


def share_product(left, right, tile=512):
    return pl.pallas_call(
        share_kernel,
        grid=(right.shape[1] // tile,),
        in_specs=[
            pl.BlockSpec(left.shape, lambda j: (0, 0)),
            pl.BlockSpec((right.shape[0], tile), lambda j: (0, j)),
        ],
        out_specs=pl.BlockSpec((left.shape[0], tile), lambda j: (0, j)),
        out_shape=jax.ShapeDtypeStruct((left.shape[0], right.shape[1]), bf16),
        compiler_params=pltpu.CompilerParams(vmem_limit_bytes=vmem),
        cost_estimate=pl.CostEstimate(
            flops=2 * left.size * right.shape[1], bytes_accessed=2 * right.size, transcendentals=0
        ),
    )(left, right)


def small_kernel(place, *refs):
    messages, inputs, down, up = refs[:ring], refs[ring], refs[ring + 1], refs[ring + 2]
    held, weights, sems = refs[ring + 3 :]
    tok = inputs.shape[0]
    width = held.shape[2]
    rank = weights.shape[1]
    copies = []
    for k, ref in enumerate(messages):
        own = pl.ds(pl.multiple_of(place[0] * tok, tok), tok)
        copies.append(pltpu.make_async_copy(ref.at[own], held.at[k], sems.at[0, k]))
        copies.append(pltpu.make_async_copy(ref.at[pl.ds(ring * tok, rank)], weights.at[k], sems.at[1, k]))
    run_all(copies)
    both = [nt(weights[k], held[k]) for k in range(ring)]
    delta = (adapter_scale * ((both[0] + both[2]) + (both[1] + both[3]))).astype(bf16)
    up[...] = delta
    down[...] = mm(delta, inputs[...])


def small_terms(messages, inputs, place):
    tok, width = inputs.shape
    rank = 16
    return pl.pallas_call(
        small_kernel,
        grid_spec=pltpu.PrefetchScalarGridSpec(
            num_scalar_prefetch=1,
            grid=(1,),
            in_specs=[hbm] * ring + [pl.BlockSpec((tok, width), lambda j, o: (0, 0))],
            out_specs=[
                pl.BlockSpec((rank, width), lambda j, o: (0, 0)),
                pl.BlockSpec((rank, tok), lambda j, o: (0, 0)),
            ],
            scratch_shapes=[
                pltpu.VMEM((ring, tok, messages[0].shape[1]), bf16),
                pltpu.VMEM((ring, rank, messages[0].shape[1]), bf16),
                pltpu.SemaphoreType.DMA((2, ring)),
            ],
        ),
        out_shape=[jax.ShapeDtypeStruct((rank, width), f32), jax.ShapeDtypeStruct((rank, tok), bf16)],
        compiler_params=pltpu.CompilerParams(vmem_limit_bytes=vmem),
        cost_estimate=light,
    )(place, *messages, inputs)


def stack(pairs, held, sems):
    copies = []
    at = 0
    for n, (ref, size) in enumerate(pairs):
        copies.append(pltpu.make_async_copy(ref.at[pl.ds(0, size)], held.at[pl.ds(at, size)], sems.at[n]))
        copies[-1].start()
        at += size
    return copies


def turn(held, offsets, turned):
    for i in range(ring):
        start = pl.multiple_of(offsets[i], lane)
        turned[i * lane : (i + 1) * lane] = held[:, pl.ds(start, lane)].T


def gradient_kernel(numbers, *refs):
    own, sibling, outs = refs[:ring], refs[ring : 2 * ring], refs[2 * ring : 3 * ring]
    held, low, turned, staged, sems, low_sems, out_sems = refs[3 * ring :]
    tok, width = held.shape[1] // 2, held.shape[2]
    sub = ring * lane
    rank = low.shape[0]
    arrivals = [stack(((own[j], tok), (sibling[j], tok)), held.at[j], sems.at[j]) for j in range(ring)]
    more = []
    for half, refs_of in enumerate((own, sibling)):
        for j in range(ring):
            start = pl.multiple_of(half * tok + numbers[2 * ring + j], lane)
            more.append(
                pltpu.make_async_copy(
                    refs_of[j].at[pl.ds(tok + rank, rank), pl.ds(0, lane)],
                    low.at[:, pl.ds(start, lane)],
                    low_sems.at[half, j],
                )
            )
            more[-1].start()
    for j in range(ring):
        for copy in arrivals[j]:
            copy.wait()
        turn(held.at[j], numbers, turned)
        for i in range(2):
            part = slice(i * width // 2, (i + 1) * width // 2)
            staged[numbers[ring + j], :sub, part] = mm(turned[...], held[0, :, part]).astype(bf16)
    for copy in more:
        copy.wait()
    extra = mm(low[...], held[0]).astype(bf16)
    for k in range(ring):
        staged[k, sub:] = extra
    run_all([pltpu.make_async_copy(staged.at[k], outs[k], out_sems.at[k]) for k in range(ring)])


def gradient_pieces(own, sibling, numbers, tok):
    width = own[0].shape[1]
    sub = ring * lane
    rank = (own[0].shape[0] - tok) // 2
    return pl.pallas_call(
        gradient_kernel,
        grid_spec=pltpu.PrefetchScalarGridSpec(
            num_scalar_prefetch=1,
            grid=(1,),
            in_specs=[hbm] * (2 * ring),
            out_specs=[hbm] * ring,
            scratch_shapes=[
                pltpu.VMEM((ring, 2 * tok, width), bf16),
                pltpu.VMEM((rank, 2 * tok), bf16),
                pltpu.VMEM((sub, 2 * tok), bf16),
                pltpu.VMEM((ring, sub + rank, width), bf16),
                pltpu.SemaphoreType.DMA((ring, 2)),
                pltpu.SemaphoreType.DMA((2, ring)),
                pltpu.SemaphoreType.DMA((ring,)),
            ],
        ),
        out_shape=[jax.ShapeDtypeStruct((sub + rank, width), bf16)] * ring,
        compiler_params=pltpu.CompilerParams(vmem_limit_bytes=vmem),
        cost_estimate=light,
    )(numbers, *own, *sibling)


def activation_kernel(tile, numbers, *refs):
    count = len(refs) - ring - 8
    pieces, extra, outs = refs[:count], refs[count : count + 2], refs[count + 2 : count + 2 + ring]
    held, turned, staged, more, sems, out_sems = refs[count + 2 + ring :]
    width = held.shape[1]
    arrivals = stack([(ref, ref.shape[0]) for ref in pieces], held, sems)
    rest = [pltpu.make_async_copy(ref, more.at[i], sems.at[count + i]) for i, ref in enumerate(extra)]
    for copy in rest:
        copy.start()
    for copy in arrivals:
        copy.wait()
    turn(held, numbers, turned)
    for copy in rest:
        copy.wait()
    term = (more[0] + more[1]).astype(bf16)
    for k in range(ring):
        staged[k, lane:] = term
    sent = []
    for j in range(width // tile):
        part = slice(j * tile, (j + 1) * tile)
        result = mm(turned[...], held[:, part]).astype(bf16)
        for k in range(ring):
            staged[k, :lane, part] = result[k * lane : (k + 1) * lane]
            sent.append(pltpu.make_async_copy(staged.at[k, :, part], outs[k].at[:, part], out_sems.at[j, k]))
            sent[-1].start()
    for copy in sent:
        copy.wait()


def activation_pieces(pieces, extra, numbers, tile=512):
    count, width = len(pieces), pieces[0].shape[1]
    tokens = sum(piece.shape[0] for piece in pieces)
    rank = extra[0].shape[0]
    return pl.pallas_call(
        functools.partial(activation_kernel, tile),
        grid_spec=pltpu.PrefetchScalarGridSpec(
            num_scalar_prefetch=1,
            grid=(1,),
            in_specs=[hbm] * (count + 2),
            out_specs=[hbm] * ring,
            scratch_shapes=[
                pltpu.VMEM((tokens, width), bf16),
                pltpu.VMEM((ring * lane, tokens), bf16),
                pltpu.VMEM((ring, lane + rank, width), bf16),
                pltpu.VMEM((2, rank, width), f32),
                pltpu.SemaphoreType.DMA((count + 2,)),
                pltpu.SemaphoreType.DMA((width // tile, ring)),
            ],
        ),
        out_shape=[jax.ShapeDtypeStruct((lane + rank, width), bf16)] * ring,
        compiler_params=pltpu.CompilerParams(vmem_limit_bytes=vmem),
        cost_estimate=light,
    )(numbers, *pieces, *extra)


def per_device(inputs, output_gradient, frozen, down, up):
    x, y, z, c = (lax.axis_index(name) for name in "xyzc")
    total = inputs.shape[0] * 128
    tok, width = output_gradient.shape
    own_rows = tok // ring
    rank = down.shape[0]
    steps = jnp.arange(ring, dtype=jnp.int32)
    ahead = jnp.where(c == 0, steps, -steps)
    row_offsets = y * width + (z + ahead) % ring * (2 * lane) + c * lane
    slots = (jnp.where(c == 0, x - y, y - x) + steps) % ring
    numbers = jnp.concatenate([(2 * steps + c) * lane, slots, (x + ahead) % ring * lane])

    x_behind, x_ahead = travel(inputs, "y", 1), travel(inputs, "y", -1)
    low = jnp.pad(nt(down, inputs).astype(bf16), ((0, 0), (0, width - inputs.shape[0])))
    message = jnp.concatenate([output_gradient, up, low], 0)
    message_behind, message_ahead = travel(message, "x", 1), travel(message, "x", -1)
    sibling_message, sibling_inputs = shift(message, "c", 1), shift(inputs, "c", 1)
    share = share_product(output_gradient, frozen).reshape(ring, own_rows, -1)
    message_behind, message_ahead, x_behind, x_ahead, sibling_message, sibling_inputs, numbers, row_offsets = together(
        message_behind, message_ahead, x_behind, x_ahead, sibling_message, sibling_inputs, numbers, row_offsets
    )
    message_far = travel(message_behind, "x", 1)
    x_far = travel(x_behind, "y", 1)
    message_far, x_far, share = together(message_far, x_far, share)
    messages = [message, message_ahead, message_far, message_behind]
    sibling_messages = [sibling_message] + [shift(messages[-k], "c", 1) for k in range(1, ring)]
    tokens = [inputs, x_ahead, x_behind, x_far]
    sibling_tokens = [sibling_inputs] + [shift(piece, "c", 1) for piece in tokens[1:]]

    down_part, delta = small_terms(messages, inputs, x.reshape(1))
    down_part = [down_part, shift(down_part, "c", 1)]
    grad = gradient_pieces(messages, sibling_messages, numbers, tok)
    *down_part, _ = together(*down_part, grad[0])
    act = activation_pieces(tokens + sibling_tokens, down_part, row_offsets)

    grad_back, grad_far = travel(grad[3], "y", -1), travel(grad[2], "y", 1)
    act_back, act_far = travel(act[3], "z", -1), travel(act[2], "z", 1)
    grad_far, act_far = together(grad_far, act_far)
    grad_front = travel((grad[1].astype(f32) + grad_far.astype(f32)).astype(bf16), "y", 1)
    act_front = travel((act[1].astype(f32) + act_far.astype(f32)).astype(bf16), "z", 1)
    share, *_ = together(share, grad[0], act[0])
    shares = lax.all_to_all(share, "x", 0, 0)
    grad_front, grad_back, act_front, act_back, shares = together(grad_front, grad_back, act_front, act_back, shares)

    def total_of(*got):
        return sum(piece.astype(f32) for piece in got)

    def places(at):
        return [(at + ahead[k]) % ring for k in range(ring)]

    reduced = total_of(act[0], act_front, act_back)
    pieces = [cols(reduced, at * width, width) for at in places(x)]
    pieces = [pieces[0]] + [travel(pieces[k].astype(bf16), "x", k) for k in (1, 3, 2)]
    down_sum = total_of(*[piece[lane:] for piece in pieces]) / total
    act_factor = total_of(*[piece[:lane] for piece in pieces]) / total
    down_sum = down_sum + exchange(down_sum, "y", 1)
    down_sum = down_sum + exchange(down_sum, "y", 2)
    reduced = total_of(grad[0], grad_front, grad_back)
    extra = reduced[ring * lane :]
    pieces = [jnp.concatenate([rows(reduced, at * lane, lane), extra], 0) for at in places(z)]
    pieces = [pieces[0]] + [travel(pieces[k].astype(bf16), "z", k) for k in (1, 3, 2)]
    grad_factor = total_of(*[piece[:lane] for piece in pieces]) / total
    up_mean = total_of(*[piece[lane:] for piece in pieces]) * (adapter_scale / total)

    shares, _ = together(shares, pieces[1])
    input_gradient = (tn(delta, down) + jnp.sum(shares.astype(f32), 0)).astype(bf16)
    return input_gradient, act_factor, grad_factor, down_sum, up_mean


def solution(mesh):
    fine = Mesh(mesh.devices.reshape(ring, ring, 2, ring), ("y", "z", "c", "x"))
    dp = ("y", "z", "c")
    return jax.shard_map(
        per_device,
        mesh=fine,
        in_specs=(P(dp + ("x",), None), P(dp, "x"), P("x", None), P(), P(None, "x")),
        out_specs=(P(dp + ("x",), None), P(dp, "x"), P(dp, "x"), P(None, "x"), P(None, "x")),
        check_vma=False,
    )
```

profile of v0, /device:TPU:0, one launch (start us, length us, event | category | flops | bytes accessed | tf_op | source)
XLA Modules:
  0.0 170.1 jit_solution(1205339979477356117)
XLA Ops:
  9.7 12.5 %collective-permute-done.2.refs_2_ = bf16[128,4096]{1,0:T(8,128)(2,1)} collective-permute-done((bf16[128,4096]{1,0:T(8,128)(2,1)}, bf16[128,4096]{1,0:T(8,128)(2,1)}, u32[]{:S(2)}, u32[]{:S(2)}) %collective-permute-start.2) | collective-permute-done | bytes 1048608 | tf_op jit(solution)/shard_map/ppermute | solution.py:35
  23.4 3.1 %collective-permute-done.3.refs_1_ = bf16[128,4096]{1,0:T(8,128)(2,1)} collective-permute-done((bf16[128,4096]{1,0:T(8,128)(2,1)S(1)}, bf16[128,4096]{1,0:T(8,128)(2,1)}, u32[]{:S(2)}, u32[]{:S(2)}) %collective-permute-start.3) | collective-permute-done | bytes 1048608 | tf_op jit(solution)/shard_map/ppermute | solution.py:35
  26.5 3.8 %collective-permute-done.refs_3_ = bf16[544,1024]{1,0:T(8,128)(2,1)S(1)} collective-permute-done((bf16[544,1024]{1,0:T(8,128)(2,1)S(1)}, bf16[544,1024]{1,0:T(8,128)(2,1)S(1)}, u32[]{:S(2)}, u32[]{:S(2)}) %collective-permute-start) | collective-permute-done | bytes 1114144 | tf_op jit(solution)/shard_map/ppermute | solution.py:35
  35.3 10.5 %shard_map.92 = bf16[512,4096]{1,0:T(8,128)(2,1)} custom-call(bf16[512,1024]{1,0:T(8,128)(2,1)} %left.1, bf16[1024,4096]{1,0:T(8,128)(2,1)} %right.1), custom_call_target="tpu_custom_call" | custom-call | flops 4294967296 | bytes 8388608 | tf_op jit(solution)/shard_map/pallas_call | solution.py:74
  45.8 3.9 %collective-permute-done.7.refs_3_ = bf16[128,4096]{1,0:T(8,128)(2,1)} collective-permute-done((bf16[128,4096]{1,0:T(8,128)(2,1)}, bf16[128,4096]{1,0:T(8,128)(2,1)}, u32[]{:S(2)}, u32[]{:S(2)}) %collective-permute-start.7) | collective-permute-done | bytes 1048608 | tf_op jit(solution)/shard_map/ppermute | solution.py:35
  50.6 4.1 %shard_map.93 = (f32[16,4096]{1,0:T(8,128)}, bf16[16,128]{1,0:T(8,128)(2,1)}) custom-call(s32[1]{0:T(128)} %bitcast.place, bf16[544,1024]{1,0:T(8,128)(2,1)} %copy-done.1, bf16[544,1024]{1,0:T(8,128)(2,1)} %collective-permute-done.1.refs_1_, bf16[544,1024]{1,0:T(8,128)(2,1)} %collective-permute-done.6.refs_2_, bf16[544,1024]{1,0:T(8,128)(2,1)} %copy-done.3, ...), custom_call_target="tpu_custom_call" | custom-call | flops 1024 | bytes 1024 | tf_op jit(solution)/shard_map/pallas_call | solution.py:111
  56.5 10.1 %shard_map.94 = (bf16[528,1024]{1,0:T(8,128)(2,1)}, bf16[528,1024]{1,0:T(8,128)(2,1)}, bf16[528,1024]{1,0:T(8,128)(2,1)}, bf16[528,1024]{1,0:T(8,128)(2,1)}) custom-call(s32[12]{0:T(128)} %pad_add_fusion.numbers, bf16[544,1024]{1,0:T(8,128)(2,1)} %copy-done.1, bf16[544,1024]{1,0:T(8,128)(2,1)} %collective-permute-done.1.refs_1_, ...), custom_call_target="tpu_custom_call" | custom-call | flops 1024 | bytes 1024 | tf_op jit(solution)/shard_map/pallas_call | solution.py:187
  68.2 10.0 %shard_map.95 = (bf16[144,4096]{1,0:T(8,128)(2,1)}, bf16[144,4096]{1,0:T(8,128)(2,1)}, bf16[144,4096]{1,0:T(8,128)(2,1)}, bf16[144,4096]{1,0:T(8,128)(2,1)}) custom-call(s32[4]{0:T(128)} %fusion.12.numbers, bf16[128,4096]{1,0:T(8,128)(2,1)} %refs_0_.1, bf16[128,4096]{1,0:T(8,128)(2,1)} %collective-permute-done.3.refs_1_, ...), custom_call_target="tpu_custom_call" | custom-call | flops 1024 | bytes 1024 | tf_op jit(solution)/shard_map/pallas_call | solution.py:243
  78.3 2.0 %collective-permute-start.16 = (bf16[144,4096]{1,0:T(8,128)(2,1)}, bf16[144,4096]{1,0:T(8,128)(2,1)S(1)}, u32[]{:S(2)}, u32[]{:S(2)}) collective-permute-start(bf16[144,4096]{1,0:T(8,128)(2,1)} %get-tuple-element.54), channel_id=1, source_target_pairs={{0,8},{4,28},{8,16},{12,4},{16,24},{20,12},{24,0},{28,20},{1,9},{5... | collective-permute-start | bytes 3538952 | tf_op jit(solution)/shard_map/ppermute | solution.py:35
  81.5 5.0 %all-to-all-start = ((bf16[4,128,4096]{2,1,0:T(8,128)(2,1)}), bf16[4,128,4096]{2,1,0:T(8,128)(2,1)}, u32[]{:S(2)}, u32[]{:S(2)}) async-start(bf16[4,128,4096]{2,1,0:T(8,128)(2,1)} %bitcast.10), calls=%async_computation | async-start | bytes 8388608 | tf_op jit(solution)/shard_map/all_to_all | solution.py:306
  86.5 2.3 %collective-permute-start.18 = (bf16[528,1024]{1,0:T(8,128)(2,1)}, bf16[528,1024]{1,0:T(8,128)(2,1)}, u32[]{:S(2)}, u32[]{:S(2)}) collective-permute-start(bf16[528,1024]{1,0:T(8,128)(2,1)} %get-tuple-element.56), channel_id=1, source_target_pairs={{0,96},{4,36},{32,0},{36,68},{64,32},{68,100},{96,64},{100,4},{1,9... | collective-permute-start | bytes 3244040 | tf_op jit(solution)/shard_map/ppermute | solution.py:35
  88.8 2.2 %collective-permute-start.20 = (bf16[144,4096]{1,0:T(8,128)(2,1)}, bf16[144,4096]{1,0:T(8,128)(2,1)}, u32[]{:S(2)}, u32[]{:S(2)}) collective-permute-start(bf16[144,4096]{1,0:T(8,128)(2,1)} %get-tuple-element.59), channel_id=1, source_target_pairs={{0,24},{4,12},{8,0},{12,20},{16,8},{20,28},{24,16},{28,4},{1,25},{... | collective-permute-start | bytes 3538952 | tf_op jit(solution)/shard_map/ppermute | solution.py:35
  91.0 10.7 %collective-permute-done.11 = bf16[528,1024]{1,0:T(8,128)(2,1)} collective-permute-done((bf16[528,1024]{1,0:T(8,128)(2,1)}, bf16[528,1024]{1,0:T(8,128)(2,1)}, u32[]{:S(2)}, u32[]{:S(2)}) %collective-permute-start.11) | collective-permute-done | bytes 1081376 | tf_op jit(solution)/shard_map/ppermute | solution.py:35
  104.4 5.7 %collective-permute-start.19 = (bf16[144,4096]{1,0:T(8,128)(2,1)S(1)}, bf16[144,4096]{1,0:T(8,128)(2,1)S(1)}, u32[]{:S(2)}, u32[]{:S(2)}) collective-permute-start(bf16[144,4096]{1,0:T(8,128)(2,1)S(1)} %add_convert_fusion), channel_id=1, source_target_pairs={{0,8},{4,28},{8,16},{12,4},{16,24},{20,12},{24,0},{28,20},{1,9},{5... | collective-permute-start | bytes 3538952 | tf_op jit(solution)/shard_map/ppermute | solution.py:35
  110.1 2.7 %add_convert_fusion.1 = bf16[528,1024]{1,0:T(8,128)(2,1)} fusion(bf16[528,1024]{1,0:T(8,128)(2,1)} %collective-permute-done.11, bf16[528,1024]{1,0:T(8,128)(2,1)S(1)} %copy-done.9), kind=kLoop, calls=%fused_computation.8 | loop fusion | flops 2162688 | bytes 3244032 | tf_op jit(solution)/shard_map/convert_element_type | solution.py:303
  118.9 10.4 %collective-permute-done.17 = bf16[528,1024]{1,0:T(8,128)(2,1)} collective-permute-done((bf16[528,1024]{1,0:T(8,128)(2,1)}, bf16[528,1024]{1,0:T(8,128)(2,1)}, u32[]{:S(2)}, u32[]{:S(2)}) %collective-permute-start.17) | collective-permute-done | bytes 1081376 | tf_op jit(solution)/shard_map/ppermute | solution.py:35
  129.4 7.0 %all-to-all-done = bf16[4,128,4096]{2,1,0:T(8,128)(2,1)} async-done(((bf16[4,128,4096]{2,1,0:T(8,128)(2,1)}), bf16[4,128,4096]{2,1,0:T(8,128)(2,1)}, u32[]{:S(2)}, u32[]{:S(2)}) %all-to-all-start) | async-done | bytes 4194336 | tf_op jit(solution)/shard_map/all_to_all | solution.py:306
  136.4 2.5 %convert_add_fusion.1 = f32[528,1024]{1,0:T(8,128)S(1)} fusion(bf16[528,1024]{1,0:T(8,128)(2,1)} %collective-permute-done.18, bf16[528,1024]{1,0:T(8,128)(2,1)} %collective-permute-done.17, bf16[528,1024]{1,0:T(8,128)(2,1)} %get-tuple-element.51), kind=kLoop, calls=%fused_computation.7 | loop fusion | flops 2703360 | bytes 5406720 | tf_op jit(solution)/shard_map/add | solution.py:310
  142.9 2.7 %collective-permute-start.23 = (bf16[144,1024]{1,0:T(8,128)(2,1)S(1)}, bf16[144,1024]{1,0:T(8,128)(2,1)S(1)}, u32[]{:S(2)}, u32[]{:S(2)}) collective-permute-start(bf16[144,1024]{1,0:T(8,128)(2,1)S(1)} %get-tuple-element.71), channel_id=1, source_target_pairs={{0,3},{4,5},{1,0},{5,6},{2,1},{6,7},{3,2},{7,4},{8,11},{12,13},{9,... | collective-permute-start | bytes 884744 | tf_op jit(solution)/shard_map/ppermute | solution.py:35
  148.3 3.2 %convert_reduce_fusion = f32[128,4096]{1,0:T(8,128)S(1)} fusion(bf16[4,128,4096]{2,1,0:T(8,128)(2,1)} %all-to-all-done), kind=kLoop, calls=%fused_computation | loop fusion | flops 3670016 | bytes 6291456 | tf_op jit(solution)/shard_map/reduce_sum | solution.py:330
  151.6 2.1 %collective-permute-done.24 = bf16[144,1024]{1,0:T(8,128)(2,1)S(1)} collective-permute-done((bf16[144,1024]{1,0:T(8,128)(2,1)S(1)}, bf16[144,1024]{1,0:T(8,128)(2,1)S(1)}, u32[]{:S(2)}, u32[]{:S(2)}) %collective-permute-start.24) | collective-permute-done | bytes 294944 | tf_op jit(solution)/shard_map/ppermute | solution.py:35
  153.7 4.1 %collective-permute-done.23 = bf16[144,1024]{1,0:T(8,128)(2,1)S(1)} collective-permute-done((bf16[144,1024]{1,0:T(8,128)(2,1)S(1)}, bf16[144,1024]{1,0:T(8,128)(2,1)S(1)}, u32[]{:S(2)}, u32[]{:S(2)}) %collective-permute-start.23) | collective-permute-done | bytes 294944 | tf_op jit(solution)/shard_map/ppermute | solution.py:35
  163.6 3.0 %collective-permute-start.28 = (f32[16,1024]{1,0:T(8,128)S(1)}, f32[16,1024]{1,0:T(8,128)S(1)}, u32[]{:S(2)}, u32[]{:S(2)}) collective-permute-start(f32[16,1024]{1,0:T(8,128)S(1)} %add.243), channel_id=1, source_target_pairs={{0,64},{32,96},{64,0},{96,32},{1,65},{33,97},{65,1},{97,33},{2,66}... | collective-permute-start | bytes 196616 | tf_op jit(solution)/shard_map/ppermute | solution.py:26
  167.2 2.2 %collective-permute-done.28 = f32[16,1024]{1,0:T(8,128)S(1)} collective-permute-done((f32[16,1024]{1,0:T(8,128)S(1)}, f32[16,1024]{1,0:T(8,128)S(1)}, u32[]{:S(2)}, u32[]{:S(2)}) %collective-permute-start.28) | collective-permute-done | bytes 65568 | tf_op jit(solution)/shard_map/ppermute | solution.py:26
  (94 shorter events, 38.2 us)
Async XLA Ops:
  0.7 21.5 %collective-permute-start.2 = (bf16[128,4096]{1,0:T(8,128)(2,1)}, bf16[128,4096]{1,0:T(8,128)(2,1)}, u32[]{:S(2)}, u32[]{:S(2)}) collective-permute-start(bf16[128,4096]{1,0:T(8,128)(2,1)} %refs_0_.1), channel_id=1, source_target_pairs={{0,32},{4,100},{32,64},{36,4},{64,96},{68,36},{96,0},{100,68},{1,3... | collective-permute-start | bytes 3145736 | tf_op jit(solution)/shard_map/ppermute | solution.py:35
  4.2 26.2 %collective-permute-start = (bf16[544,1024]{1,0:T(8,128)(2,1)S(1)}, bf16[544,1024]{1,0:T(8,128)(2,1)S(1)}, u32[]{:S(2)}, u32[]{:S(2)}) collective-permute-start(bf16[544,1024]{1,0:T(8,128)(2,1)S(1)} %fusion.2.refs_0_), channel_id=1, source_target_pairs={{0,1},{4,7},{1,2},{5,4},{2,3},{6,5},{3,0},{7,6},{8,9},{12,15},{9,1... | collective-permute-start | bytes 3342344 | tf_op jit(solution)/shard_map/ppermute | solution.py:35
  5.7 26.2 %collective-permute-start.1 = (bf16[544,1024]{1,0:T(8,128)(2,1)S(1)}, bf16[544,1024]{1,0:T(8,128)(2,1)}, u32[]{:S(2)}, u32[]{:S(2)}) collective-permute-start(bf16[544,1024]{1,0:T(8,128)(2,1)S(1)} %fusion.2.refs_0_), channel_id=1, source_target_pairs={{0,3},{4,5},{1,0},{5,6},{2,1},{6,7},{3,2},{7,4},{8,11},{12,13},{9,... | collective-permute-start | bytes 3342344 | tf_op jit(solution)/shard_map/ppermute | solution.py:35
  7.5 24.5 %collective-permute-start.4 = (bf16[544,1024]{1,0:T(8,128)(2,1)S(1)}, bf16[544,1024]{1,0:T(8,128)(2,1)}, u32[]{:S(2)}, u32[]{:S(2)}) collective-permute-start(bf16[544,1024]{1,0:T(8,128)(2,1)S(1)} %fusion.2.refs_0_), channel_id=1, source_target_pairs={{0,4},{4,0},{1,5},{5,1},{2,6},{6,2},{3,7},{7,3},{8,12},{12,8},{9,1... | collective-permute-start | bytes 3342344 | tf_op jit(solution)/shard_map/ppermute | solution.py:22
  7.7 18.8 %collective-permute-start.3 = (bf16[128,4096]{1,0:T(8,128)(2,1)S(1)}, bf16[128,4096]{1,0:T(8,128)(2,1)}, u32[]{:S(2)}, u32[]{:S(2)}) collective-permute-start(bf16[128,4096]{1,0:T(8,128)(2,1)S(1)} %copy-done.2), channel_id=1, source_target_pairs={{0,96},{4,36},{32,0},{36,68},{64,32},{68,100},{96,64},{100,4},{1,9... | collective-permute-start | bytes 3145736 | tf_op jit(solution)/shard_map/ppermute | solution.py:35
  32.0 17.6 %collective-permute-start.6 = (bf16[544,1024]{1,0:T(8,128)(2,1)S(1)}, bf16[544,1024]{1,0:T(8,128)(2,1)}, u32[]{:S(2)}, u32[]{:S(2)}) collective-permute-start(bf16[544,1024]{1,0:T(8,128)(2,1)S(1)} %collective-permute-done.refs_3_), channel_id=1, source_target_pairs={{0,1},{4,7},{1,2},{5,4},{2,3},{6,5},{3,0},{7,6},{8,9},{12,15},{9,1... | collective-permute-start | bytes 3342344 | tf_op jit(solution)/shard_map/ppermute | solution.py:35
  33.3 16.3 %collective-permute-start.7 = (bf16[128,4096]{1,0:T(8,128)(2,1)}, bf16[128,4096]{1,0:T(8,128)(2,1)}, u32[]{:S(2)}, u32[]{:S(2)}) collective-permute-start(bf16[128,4096]{1,0:T(8,128)(2,1)} %collective-permute-done.2.refs_2_), channel_id=1, source_target_pairs={{0,32},{4,100},{32,64},{36,4},{64,96},{68,36},{96,0},{100,68},{1,3... | collective-permute-start | bytes 3145736 | tf_op jit(solution)/shard_map/ppermute | solution.py:35
  34.1 16.0 %collective-permute-start.8 = (bf16[544,1024]{1,0:T(8,128)(2,1)S(1)}, bf16[544,1024]{1,0:T(8,128)(2,1)S(1)}, u32[]{:S(2)}, u32[]{:S(2)}) collective-permute-start(bf16[544,1024]{1,0:T(8,128)(2,1)S(1)} %collective-permute-done.refs_3_), channel_id=1, source_target_pairs={{0,4},{4,0},{1,5},{5,1},{2,6},{6,2},{3,7},{7,3},{8,12},{12,8},{9,1... | collective-permute-start | bytes 3342344 | tf_op jit(solution)/shard_map/ppermute | solution.py:22
  35.3 19.5 %collective-permute-start.10 = (bf16[544,1024]{1,0:T(8,128)(2,1)}, bf16[544,1024]{1,0:T(8,128)(2,1)}, u32[]{:S(2)}, u32[]{:S(2)}) collective-permute-start(bf16[544,1024]{1,0:T(8,128)(2,1)} %collective-permute-done.1.refs_1_), channel_id=1, source_target_pairs={{0,4},{4,0},{1,5},{5,1},{2,6},{6,2},{3,7},{7,3},{8,12},{12,8},{9,1... | collective-permute-start | bytes 3342344 | tf_op jit(solution)/shard_map/ppermute | solution.py:22
  49.6 16.9 %collective-permute-start.13 = (bf16[128,4096]{1,0:T(8,128)(2,1)}, bf16[128,4096]{1,0:T(8,128)(2,1)}, u32[]{:S(2)}, u32[]{:S(2)}) collective-permute-start(bf16[128,4096]{1,0:T(8,128)(2,1)} %collective-permute-done.2.refs_2_), channel_id=1, source_target_pairs={{0,4},{4,0},{1,5},{5,1},{2,6},{6,2},{3,7},{7,3},{8,12},{12,8},{9,1... | collective-permute-start | bytes 3145736 | tf_op jit(solution)/shard_map/ppermute | solution.py:22
  50.1 16.4 %collective-permute-start.12 = (bf16[128,4096]{1,0:T(8,128)(2,1)}, bf16[128,4096]{1,0:T(8,128)(2,1)}, u32[]{:S(2)}, u32[]{:S(2)}) collective-permute-start(bf16[128,4096]{1,0:T(8,128)(2,1)} %collective-permute-done.3.refs_1_), channel_id=1, source_target_pairs={{0,4},{4,0},{1,5},{5,1},{2,6},{6,2},{3,7},{7,3},{8,12},{12,8},{9,1... | collective-permute-start | bytes 3145736 | tf_op jit(solution)/shard_map/ppermute | solution.py:22
  50.1 16.4 %collective-permute-start.14 = (bf16[128,4096]{1,0:T(8,128)(2,1)}, bf16[128,4096]{1,0:T(8,128)(2,1)S(1)}, u32[]{:S(2)}, u32[]{:S(2)}) collective-permute-start(bf16[128,4096]{1,0:T(8,128)(2,1)} %collective-permute-done.7.refs_3_), channel_id=1, source_target_pairs={{0,4},{4,0},{1,5},{5,1},{2,6},{6,2},{3,7},{7,3},{8,12},{12,8},{9,1... | collective-permute-start | bytes 3145736 | tf_op jit(solution)/shard_map/ppermute | solution.py:22
  54.8 11.7 %collective-permute-start.15 = (f32[16,4096]{1,0:T(8,128)}, f32[16,4096]{1,0:T(8,128)S(1)}, u32[]{:S(2)}, u32[]{:S(2)}) collective-permute-start(f32[16,4096]{1,0:T(8,128)} %get-tuple-element.52.refs_8_), channel_id=1, source_target_pairs={{0,4},{4,0},{1,5},{5,1},{2,6},{6,2},{3,7},{7,3},{8,12},{12,8},{9,1... | collective-permute-start | bytes 786440 | tf_op jit(solution)/shard_map/ppermute | solution.py:22
  78.3 23.4 %collective-permute-start.16 = (bf16[144,4096]{1,0:T(8,128)(2,1)}, bf16[144,4096]{1,0:T(8,128)(2,1)S(1)}, u32[]{:S(2)}, u32[]{:S(2)}) collective-permute-start(bf16[144,4096]{1,0:T(8,128)(2,1)} %get-tuple-element.54), channel_id=1, source_target_pairs={{0,8},{4,28},{8,16},{12,4},{16,24},{20,12},{24,0},{28,20},{1,9},{5... | collective-permute-start | bytes 3538952 | tf_op jit(solution)/shard_map/ppermute | solution.py:35
  80.3 21.4 %collective-permute-start.11 = (bf16[528,1024]{1,0:T(8,128)(2,1)}, bf16[528,1024]{1,0:T(8,128)(2,1)}, u32[]{:S(2)}, u32[]{:S(2)}) collective-permute-start(bf16[528,1024]{1,0:T(8,128)(2,1)} %get-tuple-element.45), channel_id=1, source_target_pairs={{0,32},{4,100},{32,64},{36,4},{64,96},{68,36},{96,0},{100,68},{1,3... | collective-permute-start | bytes 3244040 | tf_op jit(solution)/shard_map/ppermute | solution.py:35
  81.5 54.9 %all-to-all-start = ((bf16[4,128,4096]{2,1,0:T(8,128)(2,1)}), bf16[4,128,4096]{2,1,0:T(8,128)(2,1)}, u32[]{:S(2)}, u32[]{:S(2)}) async-start(bf16[4,128,4096]{2,1,0:T(8,128)(2,1)} %bitcast.10), calls=%async_computation | async-start | bytes 8388608 | tf_op jit(solution)/shard_map/all_to_all | solution.py:306
  86.5 32.4 %collective-permute-start.18 = (bf16[528,1024]{1,0:T(8,128)(2,1)}, bf16[528,1024]{1,0:T(8,128)(2,1)}, u32[]{:S(2)}, u32[]{:S(2)}) collective-permute-start(bf16[528,1024]{1,0:T(8,128)(2,1)} %get-tuple-element.56), channel_id=1, source_target_pairs={{0,96},{4,36},{32,0},{36,68},{64,32},{68,100},{96,64},{100,4},{1,9... | collective-permute-start | bytes 3244040 | tf_op jit(solution)/shard_map/ppermute | solution.py:35
  88.8 30.1 %collective-permute-start.20 = (bf16[144,4096]{1,0:T(8,128)(2,1)}, bf16[144,4096]{1,0:T(8,128)(2,1)}, u32[]{:S(2)}, u32[]{:S(2)}) collective-permute-start(bf16[144,4096]{1,0:T(8,128)(2,1)} %get-tuple-element.59), channel_id=1, source_target_pairs={{0,24},{4,12},{8,0},{12,20},{16,8},{20,28},{24,16},{28,4},{1,25},{... | collective-permute-start | bytes 3538952 | tf_op jit(solution)/shard_map/ppermute | solution.py:35
  104.4 25.0 %collective-permute-start.19 = (bf16[144,4096]{1,0:T(8,128)(2,1)S(1)}, bf16[144,4096]{1,0:T(8,128)(2,1)S(1)}, u32[]{:S(2)}, u32[]{:S(2)}) collective-permute-start(bf16[144,4096]{1,0:T(8,128)(2,1)S(1)} %add_convert_fusion), channel_id=1, source_target_pairs={{0,8},{4,28},{8,16},{12,4},{16,24},{20,12},{24,0},{28,20},{1,9},{5... | collective-permute-start | bytes 3538952 | tf_op jit(solution)/shard_map/ppermute | solution.py:35
  112.7 16.7 %collective-permute-start.17 = (bf16[528,1024]{1,0:T(8,128)(2,1)}, bf16[528,1024]{1,0:T(8,128)(2,1)}, u32[]{:S(2)}, u32[]{:S(2)}) collective-permute-start(bf16[528,1024]{1,0:T(8,128)(2,1)} %add_convert_fusion.1), channel_id=1, source_target_pairs={{0,32},{4,100},{32,64},{36,4},{64,96},{68,36},{96,0},{100,68},{1,3... | collective-permute-start | bytes 3244040 | tf_op jit(solution)/shard_map/ppermute | solution.py:35
  142.9 14.9 %collective-permute-start.23 = (bf16[144,1024]{1,0:T(8,128)(2,1)S(1)}, bf16[144,1024]{1,0:T(8,128)(2,1)S(1)}, u32[]{:S(2)}, u32[]{:S(2)}) collective-permute-start(bf16[144,1024]{1,0:T(8,128)(2,1)S(1)} %get-tuple-element.71), channel_id=1, source_target_pairs={{0,3},{4,5},{1,0},{5,6},{2,1},{6,7},{3,2},{7,4},{8,11},{12,13},{9,... | collective-permute-start | bytes 884744 | tf_op jit(solution)/shard_map/ppermute | solution.py:35
  145.6 13.7 %collective-permute-start.22 = (bf16[144,1024]{1,0:T(8,128)(2,1)S(1)}, bf16[144,1024]{1,0:T(8,128)(2,1)S(1)}, u32[]{:S(2)}, u32[]{:S(2)}) collective-permute-start(bf16[144,1024]{1,0:T(8,128)(2,1)S(1)} %get-tuple-element.69), channel_id=1, source_target_pairs={{0,1},{4,7},{1,2},{5,4},{2,3},{6,5},{3,0},{7,6},{8,9},{12,15},{9,1... | collective-permute-start | bytes 884744 | tf_op jit(solution)/shard_map/ppermute | solution.py:35
  145.6 17.0 %collective-permute-start.26 = (bf16[144,1024]{1,0:T(8,128)(2,1)S(1)}, bf16[144,1024]{1,0:T(8,128)(2,1)S(1)}, u32[]{:S(2)}, u32[]{:S(2)}) collective-permute-start(bf16[144,1024]{1,0:T(8,128)(2,1)S(1)} %get-tuple-element.76), channel_id=1, source_target_pairs={{0,16},{4,20},{8,24},{12,28},{16,0},{20,4},{24,8},{28,12},{1,17},{... | collective-permute-start | bytes 884744 | tf_op jit(solution)/shard_map/ppermute | solution.py:35
  147.4 15.2 %collective-permute-start.25 = (bf16[144,1024]{1,0:T(8,128)(2,1)S(1)}, bf16[144,1024]{1,0:T(8,128)(2,1)S(1)}, u32[]{:S(2)}, u32[]{:S(2)}) collective-permute-start(bf16[144,1024]{1,0:T(8,128)(2,1)S(1)} %get-tuple-element.75), channel_id=1, source_target_pairs={{0,24},{4,12},{8,0},{12,20},{16,8},{20,28},{24,16},{28,4},{1,25},{... | collective-permute-start | bytes 884744 | tf_op jit(solution)/shard_map/ppermute | solution.py:35
  (21 other events, 157.1 us)
where the time goes:
time: 171 us; the launch traced here: 170 us
  waiting for transfers between devices  63.1 us (37%)
  starting transfers between devices  41.3 us (24%)
  Pallas kernels  34.7 us (20%)
  other arithmetic  16.3 us (10%)
  between operations  6.21 us (4%)
  local copies, waits for them, and re-layouts  5.52 us (3%)
  matrix products  3.05 us (2%)
    ppermute x18, waiting for transfers between devices, travel(): return lax.ppermute(array, order, pairs)  53.7 us
    ppermute x18, starting transfers between devices, travel(): return lax.ppermute(array, order, pairs)  29.3 us
    pallas_call x1, Pallas kernels, share_product(): pl.pallas_call(share_kernel, grid=(right.shape[1] // tile,), in_specs=[pl...  10.5 us
    pallas_call x1, Pallas kernels, gradient_pieces(): pl.pallas_call(gradient_kernel, grid_spec=pltpu.PrefetchScalarGridSpec(nu...  10.1 us
    pallas_call x1, Pallas kernels, activation_pieces(): pl.pallas_call(functools.partial(activation_kernel, tile), grid_spec=pltp...  10 us
    all_to_all x1, waiting for transfers between devices, per_device(): shares = lax.all_to_all(share, 'x', 0, 0)  7 us
    all_to_all x1, starting transfers between devices, per_device(): shares = lax.all_to_all(share, 'x', 0, 0)  4.98 us
    unnamed x30, local copies, waits for them, and re-layouts  4.61 us
  transfers between devices with their start and end apart: 30, of which 13 were waited for; matrix products, arithmetic and copies ran while one was open for 10% of the time, Pallas kernels for 14%

commit v1 on v0

--- a/solution.py
+++ b/solution.py
@@ -102,7 +102,7 @@
     both = [nt(weights[k], held[k]) for k in range(ring)]
     delta = (adapter_scale * ((both[0] + both[2]) + (both[1] + both[3]))).astype(bf16)
     up[...] = delta
-    down[...] = mm(delta, inputs[...])
+    down[...] = mm(delta, inputs[...]).astype(bf16)
 
 
 def small_terms(messages, inputs, place):
@@ -124,7 +124,7 @@
                 pltpu.SemaphoreType.DMA((2, ring)),
             ],
         ),
-        out_shape=[jax.ShapeDtypeStruct((rank, width), f32), jax.ShapeDtypeStruct((rank, tok), bf16)],
+        out_shape=[jax.ShapeDtypeStruct((rank, width), bf16), jax.ShapeDtypeStruct((rank, tok), bf16)],
         compiler_params=pltpu.CompilerParams(vmem_limit_bytes=vmem),
         cost_estimate=light,
     )(place, *messages, inputs)
@@ -152,11 +152,15 @@
     tok, width = held.shape[1] // 2, held.shape[2]
     sub = ring * lane
     rank = low.shape[0]
-    arrivals = [stack(((own[j], tok), (sibling[j], tok)), held.at[j], sems.at[j]) for j in range(ring)]
-    more = []
-    for half, refs_of in enumerate((own, sibling)):
-        for j in range(ring):
-            start = pl.multiple_of(half * tok + numbers[2 * ring + j], lane)
+    offset = pl.multiple_of(numbers[3 * ring], lane)
+    starts = (offset, tok - offset)
+    arrivals, more = [], []
+    for j in range(ring):
+        for half, refs_of in enumerate((own, sibling)):
+            part = pl.ds(pl.multiple_of(starts[half], lane), tok)
+            arrivals.append(pltpu.make_async_copy(refs_of[j].at[pl.ds(0, tok)], held.at[j, part], sems.at[j, half]))
+            arrivals[-1].start()
+            start = pl.multiple_of(starts[half] + numbers[2 * ring + j], lane)
             more.append(
                 pltpu.make_async_copy(
                     refs_of[j].at[pl.ds(tok + rank, rank), pl.ds(0, lane)],
@@ -165,19 +169,29 @@
                 )
             )
             more[-1].start()
+    extra = None
     for j in range(ring):
-        for copy in arrivals[j]:
+        for copy in arrivals[2 * j : 2 * j + 2]:
             copy.wait()
+        if j == 0:
+            for copy in more:
+                copy.wait()
+            extra = mm(low[...], held[0]).astype(bf16)
+            for k in range(ring):
+                staged[k, sub:] = extra
         turn(held.at[j], numbers, turned)
+        slot = numbers[ring + j]
         for i in range(2):
             part = slice(i * width // 2, (i + 1) * width // 2)
-            staged[numbers[ring + j], :sub, part] = mm(turned[...], held[0, :, part]).astype(bf16)
-    for copy in more:
-        copy.wait()
-    extra = mm(low[...], held[0]).astype(bf16)
+            staged[slot, :sub, part] = mm(turned[...], held[0, :, part]).astype(bf16)
+        for k in range(ring):
+
+            @pl.when(slot == k)
+            def _():
+                pltpu.make_async_copy(staged.at[k], outs[k], out_sems.at[k]).start()
+
     for k in range(ring):
-        staged[k, sub:] = extra
-    run_all([pltpu.make_async_copy(staged.at[k], outs[k], out_sems.at[k]) for k in range(ring)])
+        pltpu.make_async_copy(staged.at[k], outs[k], out_sems.at[k]).wait()
 
 
 def gradient_pieces(own, sibling, numbers, tok):
@@ -221,7 +235,7 @@
     turn(held, numbers, turned)
     for copy in rest:
         copy.wait()
-    term = (more[0] + more[1]).astype(bf16)
+    term = (more[0].astype(f32) + more[1].astype(f32)).astype(bf16)
     for k in range(ring):
         staged[k, lane:] = term
     sent = []
@@ -251,7 +265,7 @@
                 pltpu.VMEM((tokens, width), bf16),
                 pltpu.VMEM((ring * lane, tokens), bf16),
                 pltpu.VMEM((ring, lane + rank, width), bf16),
-                pltpu.VMEM((2, rank, width), f32),
+                pltpu.VMEM((2, rank, width), bf16),
                 pltpu.SemaphoreType.DMA((count + 2,)),
                 pltpu.SemaphoreType.DMA((width // tile, ring)),
             ],
@@ -269,10 +283,11 @@
     own_rows = tok // ring
     rank = down.shape[0]
     steps = jnp.arange(ring, dtype=jnp.int32)
-    ahead = jnp.where(c == 0, steps, -steps)
+    sign = 1 - 2 * c
+    ahead = sign * steps
     row_offsets = y * width + (z + ahead) % ring * (2 * lane) + c * lane
     slots = (jnp.where(c == 0, x - y, y - x) + steps) % ring
-    numbers = jnp.concatenate([(2 * steps + c) * lane, slots, (x + ahead) % ring * lane])
+    numbers = jnp.concatenate([(2 * steps + c) * lane, slots, (x + ahead) % ring * lane, c[None] * tok])
 
     x_behind, x_ahead = travel(inputs, "y", 1), travel(inputs, "y", -1)
     low = jnp.pad(nt(down, inputs).astype(bf16), ((0, 0), (0, width - inputs.shape[0])))
@@ -285,49 +300,60 @@
     )
     message_far = travel(message_behind, "x", 1)
     x_far = travel(x_behind, "y", 1)
-    message_far, x_far, share = together(message_far, x_far, share)
+    sibling_behind, sibling_ahead = shift(message_behind, "c", 1), shift(message_ahead, "c", 1)
+    sibling_x_behind, sibling_x_ahead = shift(x_behind, "c", 1), shift(x_ahead, "c", 1)
+    message_far, x_far, sibling_behind, sibling_ahead, sibling_x_behind, sibling_x_ahead, _ = together(
+        message_far, x_far, sibling_behind, sibling_ahead, sibling_x_behind, sibling_x_ahead, share
+    )
     messages = [message, message_ahead, message_far, message_behind]
-    sibling_messages = [sibling_message] + [shift(messages[-k], "c", 1) for k in range(1, ring)]
+    sibling_messages = [sibling_message, sibling_behind, shift(message_far, "c", 1), sibling_ahead]
     tokens = [inputs, x_ahead, x_behind, x_far]
-    sibling_tokens = [sibling_inputs] + [shift(piece, "c", 1) for piece in tokens[1:]]
+    sibling_tokens = [sibling_inputs, sibling_x_ahead, sibling_x_behind, shift(x_far, "c", 1)]
 
     down_part, delta = small_terms(messages, inputs, x.reshape(1))
     down_part = [down_part, shift(down_part, "c", 1)]
+    numbers, *down_part = together(numbers, *down_part)
     grad = gradient_pieces(messages, sibling_messages, numbers, tok)
     *down_part, _ = together(*down_part, grad[0])
     act = activation_pieces(tokens + sibling_tokens, down_part, row_offsets)
 
-    grad_back, grad_far = travel(grad[3], "y", -1), travel(grad[2], "y", 1)
-    act_back, act_far = travel(act[3], "z", -1), travel(act[2], "z", 1)
-    grad_far, act_far = together(grad_far, act_far)
-    grad_front = travel((grad[1].astype(f32) + grad_far.astype(f32)).astype(bf16), "y", 1)
-    act_front = travel((act[1].astype(f32) + act_far.astype(f32)).astype(bf16), "z", 1)
-    share, *_ = together(share, grad[0], act[0])
     shares = lax.all_to_all(share, "x", 0, 0)
-    grad_front, grad_back, act_front, act_back, shares = together(grad_front, grad_back, act_front, act_back, shares)
-
-    def total_of(*got):
-        return sum(piece.astype(f32) for piece in got)
-
-    def places(at):
-        return [(at + ahead[k]) % ring for k in range(ring)]
-
-    reduced = total_of(act[0], act_front, act_back)
-    pieces = [cols(reduced, at * width, width) for at in places(x)]
-    pieces = [pieces[0]] + [travel(pieces[k].astype(bf16), "x", k) for k in (1, 3, 2)]
+
+    def pass_on(near, far, count):
+        return jnp.concatenate([(near[:count].astype(f32) + far[:count].astype(f32)).astype(bf16), far[count:]], 0)
+
+    grad_far, grad_back = travel(grad[2], "y", 1), travel(grad[3], "y", -1)
+    act_far, act_back = travel(act[2], "z", 1), travel(act[3], "z", -1)
+    grad_next = pass_on(grad[1], grad_far, ring * lane)
+    grad_next, grad_back, act_far, act_back, shares = together(grad_next, grad_back, act_far, act_back, shares)
+    grad_front = travel(grad_next, "y", 1)
+    act_front = travel(pass_on(act[1], act_far, lane), "z", 1)
+    input_gradient = (tn(delta, down) + jnp.sum(shares.astype(f32), 0)).astype(bf16)
+    def total_of(own, far, front, back):
+        return (own.astype(f32) + far.astype(f32)) + (front.astype(f32) + back.astype(f32))
+
+    def sums_of(own, far, front, back, count):
+        factor = own[:count].astype(f32) + (front[:count].astype(f32) + back[:count].astype(f32))
+        return factor, total_of(own[count:], front[count:], far[count:], back[count:])
+
+    def spread(pieces, axis):
+        return pieces[0], *[travel(pieces[k], axis, k) for k in (2, 1, 3)]
+
+    factor, term = sums_of(grad[0], grad_far, grad_front, grad_back, ring * lane)
+    pieces = [
+        jnp.concatenate([rows(factor, (z + sign * k + ring) % ring * lane, lane), term], 0).astype(bf16) for k in range(ring)
+    ]
+    input_gradient, act_front, *pieces = together(input_gradient, act_front, *pieces)
+    pieces = spread(pieces, "z")
+    grad_factor = total_of(*[piece[:lane] for piece in pieces]) / total
+    up_mean = total_of(*[piece[lane:] for piece in pieces]) * (adapter_scale / total)
+    factor, term = sums_of(act[0], act_far, act_front, act_back, lane)
+    reduced = jnp.concatenate([factor, term], 0)
+    pieces = [cols(reduced, (x + sign * k + ring) % ring * width, width).astype(bf16) for k in range(ring)]
+    pieces = spread(pieces, "x")
     down_sum = total_of(*[piece[lane:] for piece in pieces]) / total
     act_factor = total_of(*[piece[:lane] for piece in pieces]) / total
-    down_sum = down_sum + exchange(down_sum, "y", 1)
-    down_sum = down_sum + exchange(down_sum, "y", 2)
-    reduced = total_of(grad[0], grad_front, grad_back)
-    extra = reduced[ring * lane :]
-    pieces = [jnp.concatenate([rows(reduced, at * lane, lane), extra], 0) for at in places(z)]
-    pieces = [pieces[0]] + [travel(pieces[k].astype(bf16), "z", k) for k in (1, 3, 2)]
-    grad_factor = total_of(*[piece[:lane] for piece in pieces]) / total
-    up_mean = total_of(*[piece[lane:] for piece in pieces]) * (adapter_scale / total)
-
-    shares, _ = together(shares, pieces[1])
-    input_gradient = (tn(delta, down) + jnp.sum(shares.astype(f32), 0)).astype(bf16)
+    down_sum = total_of(*spread([down_sum] * ring, "y"))
     return input_gradient, act_factor, grad_factor, down_sum, up_mean
 
 

time: 171 us -> 161 us (0.942)
  waiting for transfers between devices: 63.1 us -> 55.1 us
  starting transfers between devices: 41.3 us -> 46.8 us
  between operations: 6.21 us -> 0.94 us
    ppermute x18 -> x21, waiting for transfers between devices: 53.7 us -> 44.6 us  [travel(): return lax.ppermute(array, order, pairs)]
    ppermute x18 -> x21, starting transfers between devices: 29.3 us -> 36.2 us  [travel(): return lax.ppermute(array, order, pairs)]
    ppermute x2 -> x0, starting transfers between devices: 3.89 us -> none  [exchange(): lax.ppermute(array, axis, [(i, i ^ step) for i in range(lax.axis_size(axi...]
    ppermute x9, starting transfers between devices: 3.09 us -> 5.73 us  [shift(): lax.ppermute(array, axis, [(i, (i + step) % size) for i in range(size)])]
    ppermute x2 -> x0, waiting for transfers between devices: 2.35 us -> none  [exchange(): lax.ppermute(array, axis, [(i, i ^ step) for i in range(lax.axis_size(axi...]
    all_to_all x1, waiting for transfers between devices: 7 us -> 8.94 us  [per_device(): shares = lax.all_to_all(share, 'x', 0, 0)]
    add x4, other arithmetic: 4.91 us -> 3.06 us  [the longest x2 2.35 us: sums_of(): own[:count].astype(f32)]
    unnamed x30 -> x26, local copies, waits for them, and re-layouts: 4.61 us -> 3.22 us
  transfers between devices with their start and end apart: 30 -> 31, of which waited for: 13 -> 14; matrix products, arithmetic and copies ran while one was open for 10% -> 11% of each run, Pallas kernels for 14% -> 22%
where the time goes in v1:
time: 161 us
  waiting for transfers between devices  55.1 us (34%)
  starting transfers between devices  46.8 us (29%)
  Pallas kernels  35.1 us (22%)
  other arithmetic  15.7 us (10%)
  local copies, waits for them, and re-layouts  4.07 us (3%)
  matrix products  3.05 us (2%)
    ppermute x21, waiting for transfers between devices, travel(): return lax.ppermute(array, order, pairs)  44.6 us
    ppermute x21, starting transfers between devices, travel(): return lax.ppermute(array, order, pairs)  36.2 us
    pallas_call x1, Pallas kernels, gradient_pieces(): pl.pallas_call(gradient_kernel, grid_spec=pltpu.PrefetchScalarGridSpec(nu...  10.5 us
    pallas_call x1, Pallas kernels, share_product(): pl.pallas_call(share_kernel, grid=(right.shape[1] // tile,), in_specs=[pl...  10.4 us
    pallas_call x1, Pallas kernels, activation_pieces(): pl.pallas_call(functools.partial(activation_kernel, tile), grid_spec=pltp...  10.1 us
    all_to_all x1, waiting for transfers between devices, per_device(): shares = lax.all_to_all(share, 'x', 0, 0)  8.94 us
    ppermute x9, starting transfers between devices, shift(): lax.ppermute(array, axis, [(i, (i + step) % size) for i in range(size)])  5.73 us
    all_to_all x1, starting transfers between devices, per_device(): shares = lax.all_to_all(share, 'x', 0, 0)  4.87 us
  transfers between devices with their start and end apart: 31, of which 14 were waited for; matrix products, arithmetic and copies ran while one was open for 11% of the time, Pallas kernels for 22%

profile of v1, /device:TPU:0, one launch (start us, length us, event | category | flops | bytes accessed | tf_op | source)
XLA Modules:
  0.0 160.7 jit_solution(6617782781429660410)
XLA Ops:
  7.7 2.0 %collective-permute-start.3 = (bf16[128,4096]{1,0:T(8,128)(2,1)S(1)}, bf16[128,4096]{1,0:T(8,128)(2,1)}, u32[]{:S(2)}, u32[]{:S(2)}) collective-permute-start(bf16[128,4096]{1,0:T(8,128)(2,1)S(1)} %copy-done.2), channel_id=1, source_target_pairs={{0,96},{4,36},{32,0},{36,68},{64,32},{68,100},{96,64},{100,4},{1,9... | collective-permute-start | bytes 3145736 | tf_op jit(solution)/shard_map/ppermute | solution.py:35
  9.7 12.5 %collective-permute-done.2.refs_2_ = bf16[128,4096]{1,0:T(8,128)(2,1)} collective-permute-done((bf16[128,4096]{1,0:T(8,128)(2,1)}, bf16[128,4096]{1,0:T(8,128)(2,1)}, u32[]{:S(2)}, u32[]{:S(2)}) %collective-permute-start.2) | collective-permute-done | bytes 1048608 | tf_op jit(solution)/shard_map/ppermute | solution.py:35
  23.4 3.1 %collective-permute-done.3.refs_1_ = bf16[128,4096]{1,0:T(8,128)(2,1)} collective-permute-done((bf16[128,4096]{1,0:T(8,128)(2,1)S(1)}, bf16[128,4096]{1,0:T(8,128)(2,1)}, u32[]{:S(2)}, u32[]{:S(2)}) %collective-permute-start.3) | collective-permute-done | bytes 1048608 | tf_op jit(solution)/shard_map/ppermute | solution.py:35
  26.5 3.8 %collective-permute-done.refs_3_ = bf16[544,1024]{1,0:T(8,128)(2,1)S(1)} collective-permute-done((bf16[544,1024]{1,0:T(8,128)(2,1)S(1)}, bf16[544,1024]{1,0:T(8,128)(2,1)S(1)}, u32[]{:S(2)}, u32[]{:S(2)}) %collective-permute-start) | collective-permute-done | bytes 1114144 | tf_op jit(solution)/shard_map/ppermute | solution.py:35
  33.4 2.6 %collective-permute-start.8 = (bf16[544,1024]{1,0:T(8,128)(2,1)S(1)}, bf16[544,1024]{1,0:T(8,128)(2,1)S(1)}, u32[]{:S(2)}, u32[]{:S(2)}) collective-permute-start(bf16[544,1024]{1,0:T(8,128)(2,1)S(1)} %collective-permute-done.refs_3_), channel_id=1, source_target_pairs={{0,4},{4,0},{1,5},{5,1},{2,6},{6,2},{3,7},{7,3},{8,12},{12,8},{9,1... | collective-permute-start | bytes 3342344 | tf_op jit(solution)/shard_map/ppermute | solution.py:22
  37.3 10.4 %shard_map.92 = bf16[512,4096]{1,0:T(8,128)(2,1)} custom-call(bf16[512,1024]{1,0:T(8,128)(2,1)} %left.1, bf16[1024,4096]{1,0:T(8,128)(2,1)} %right.1), custom_call_target="tpu_custom_call" | custom-call | flops 4294967296 | bytes 8388608 | tf_op jit(solution)/shard_map/pallas_call | solution.py:74
  47.7 4.9 %all-to-all-start = ((bf16[4,128,4096]{2,1,0:T(8,128)(2,1)}), bf16[4,128,4096]{2,1,0:T(8,128)(2,1)}, u32[]{:S(2)}, u32[]{:S(2)}) async-start(bf16[4,128,4096]{2,1,0:T(8,128)(2,1)} %bitcast.7), calls=%async_computation | async-start | bytes 8388608 | tf_op jit(solution)/shard_map/all_to_all | solution.py:320
  53.3 4.1 %shard_map.93 = (bf16[16,4096]{1,0:T(8,128)(2,1)}, bf16[16,128]{1,0:T(8,128)(2,1)}) custom-call(s32[1]{0:T(128)} %bitcast.place, bf16[544,1024]{1,0:T(8,128)(2,1)} %copy-done.1, bf16[544,1024]{1,0:T(8,128)(2,1)} %collective-permute-done.1.refs_1_, bf16[544,1024]{1,0:T(8,128)(2,1)} %collective-permute-done.6.refs_2_, bf16[544,1024]{1,0:T(8,128)(2,1)} %copy-done.3, ...), custom_call_target="tpu_custom_call" | custom-call | flops 1024 | bytes 1024 | tf_op jit(solution)/shard_map/pallas_call | solution.py:111
  60.0 10.5 %shard_map.94 = (bf16[528,1024]{1,0:T(8,128)(2,1)}, bf16[528,1024]{1,0:T(8,128)(2,1)}, bf16[528,1024]{1,0:T(8,128)(2,1)}, bf16[528,1024]{1,0:T(8,128)(2,1)}) custom-call(s32[13]{0:T(128)} %pad_add_fusion.numbers, bf16[544,1024]{1,0:T(8,128)(2,1)} %copy-done.1, bf16[544,1024]{1,0:T(8,128)(2,1)} %collective-permute-done.1.refs_1_, ...), custom_call_target="tpu_custom_call" | custom-call | flops 1024 | bytes 1024 | tf_op jit(solution)/shard_map/pallas_call | solution.py:201
  72.7 10.1 %shard_map.95 = (bf16[144,4096]{1,0:T(8,128)(2,1)}, bf16[144,4096]{1,0:T(8,128)(2,1)}, bf16[144,4096]{1,0:T(8,128)(2,1)}, bf16[144,4096]{1,0:T(8,128)(2,1)}) custom-call(s32[4]{0:T(128)} %fusion.14.numbers, bf16[128,4096]{1,0:T(8,128)(2,1)} %refs_0_.1, bf16[128,4096]{1,0:T(8,128)(2,1)} %collective-permute-done.3.refs_1_, ...), custom_call_target="tpu_custom_call" | custom-call | flops 1024 | bytes 1024 | tf_op jit(solution)/shard_map/pallas_call | solution.py:257
  82.8 2.0 %collective-permute-start.17 = (bf16[144,4096]{1,0:T(8,128)(2,1)}, bf16[144,4096]{1,0:T(8,128)(2,1)S(1)}, u32[]{:S(2)}, u32[]{:S(2)}) collective-permute-start(bf16[144,4096]{1,0:T(8,128)(2,1)} %get-tuple-element.70), channel_id=1, source_target_pairs={{0,8},{4,28},{8,16},{12,4},{16,24},{20,12},{24,0},{28,20},{1,9},{5... | collective-permute-start | bytes 3538952 | tf_op jit(solution)/shard_map/ppermute | solution.py:35
  84.8 2.2 %collective-permute-start.18 = (bf16[144,4096]{1,0:T(8,128)(2,1)}, bf16[144,4096]{1,0:T(8,128)(2,1)S(1)}, u32[]{:S(2)}, u32[]{:S(2)}) collective-permute-start(bf16[144,4096]{1,0:T(8,128)(2,1)} %get-tuple-element.71), channel_id=1, source_target_pairs={{0,24},{4,12},{8,0},{12,20},{16,8},{20,28},{24,16},{28,4},{1,25},{... | collective-permute-start | bytes 3538952 | tf_op jit(solution)/shard_map/ppermute | solution.py:35
  87.0 2.2 %collective-permute-start.15 = (bf16[528,1024]{1,0:T(8,128)(2,1)}, bf16[528,1024]{1,0:T(8,128)(2,1)}, u32[]{:S(2)}, u32[]{:S(2)}) collective-permute-start(bf16[528,1024]{1,0:T(8,128)(2,1)} %get-tuple-element.59), channel_id=1, source_target_pairs={{0,96},{4,36},{32,0},{36,68},{64,32},{68,100},{96,64},{100,4},{1,9... | collective-permute-start | bytes 3244040 | tf_op jit(solution)/shard_map/ppermute | solution.py:35
  93.0 8.9 %all-to-all-done = bf16[4,128,4096]{2,1,0:T(8,128)(2,1)} async-done(((bf16[4,128,4096]{2,1,0:T(8,128)(2,1)}), bf16[4,128,4096]{2,1,0:T(8,128)(2,1)}, u32[]{:S(2)}, u32[]{:S(2)}) %all-to-all-start) | async-done | bytes 4194336 | tf_op jit(solution)/shard_map/all_to_all | solution.py:320
  102.5 8.2 %collective-permute-done.17 = bf16[144,4096]{1,0:T(8,128)(2,1)S(1)} collective-permute-done((bf16[144,4096]{1,0:T(8,128)(2,1)}, bf16[144,4096]{1,0:T(8,128)(2,1)S(1)}, u32[]{:S(2)}, u32[]{:S(2)}) %collective-permute-start.17) | collective-permute-done | bytes 1179680 | tf_op jit(solution)/shard_map/ppermute | solution.py:35
  110.7 2.8 %collective-permute-done.18 = bf16[144,4096]{1,0:T(8,128)(2,1)S(1)} collective-permute-done((bf16[144,4096]{1,0:T(8,128)(2,1)}, bf16[144,4096]{1,0:T(8,128)(2,1)S(1)}, u32[]{:S(2)}, u32[]{:S(2)}) %collective-permute-start.18) | collective-permute-done | bytes 1179680 | tf_op jit(solution)/shard_map/ppermute | solution.py:35
  115.9 3.2 %convert_reduce_fusion = f32[128,4096]{1,0:T(8,128)S(1)} fusion(bf16[4,128,4096]{2,1,0:T(8,128)(2,1)} %all-to-all-done), kind=kLoop, calls=%fused_computation | loop fusion | flops 3670016 | bytes 6291456 | tf_op jit(solution)/shard_map/reduce_sum | solution.py:331
  120.6 9.5 %collective-permute-done.20 = bf16[528,1024]{1,0:T(8,128)(2,1)S(1)} collective-permute-done((bf16[528,1024]{1,0:T(8,128)(2,1)}, bf16[528,1024]{1,0:T(8,128)(2,1)S(1)}, u32[]{:S(2)}, u32[]{:S(2)}) %collective-permute-start.20) | collective-permute-done | bytes 1081376 | tf_op jit(solution)/shard_map/ppermute | solution.py:35
  134.8 3.6 %collective-permute-start.21 = (bf16[144,1024]{1,0:T(8,128)(2,1)S(1)}, bf16[144,1024]{1,0:T(8,128)(2,1)S(1)}, u32[]{:S(2)}, u32[]{:S(2)}) collective-permute-start(bf16[144,1024]{1,0:T(8,128)(2,1)S(1)} %get-tuple-element.86), channel_id=1, source_target_pairs={{0,2},{4,6},{1,3},{5,7},{2,0},{6,4},{3,1},{7,5},{8,10},{12,14},{9,... | collective-permute-start | bytes 884744 | tf_op jit(solution)/shard_map/ppermute | solution.py:35
  138.9 2.7 %collective-permute-start.23 = (bf16[144,1024]{1,0:T(8,128)(2,1)S(1)}, bf16[144,1024]{1,0:T(8,128)(2,1)S(1)}, u32[]{:S(2)}, u32[]{:S(2)}) collective-permute-start(bf16[144,1024]{1,0:T(8,128)(2,1)S(1)} %get-tuple-element.88), channel_id=1, source_target_pairs={{0,3},{4,5},{1,0},{5,6},{2,1},{6,7},{3,2},{7,4},{8,11},{12,13},{9,... | collective-permute-start | bytes 884744 | tf_op jit(solution)/shard_map/ppermute | solution.py:35
  141.6 2.2 %collective-permute-start.24 = (bf16[144,1024]{1,0:T(8,128)(2,1)S(1)}, bf16[144,1024]{1,0:T(8,128)(2,1)S(1)}, u32[]{:S(2)}, u32[]{:S(2)}) collective-permute-start(bf16[144,1024]{1,0:T(8,128)(2,1)S(1)} %get-tuple-element.82), channel_id=1, source_target_pairs={{0,16},{4,20},{8,24},{12,28},{16,0},{20,4},{24,8},{28,12},{1,17},{... | collective-permute-start | bytes 884744 | tf_op jit(solution)/shard_map/ppermute | solution.py:35
  143.8 2.2 %collective-permute-start.25 = (bf16[144,1024]{1,0:T(8,128)(2,1)S(1)}, bf16[144,1024]{1,0:T(8,128)(2,1)S(1)}, u32[]{:S(2)}, u32[]{:S(2)}) collective-permute-start(bf16[144,1024]{1,0:T(8,128)(2,1)S(1)} %get-tuple-element.83), channel_id=1, source_target_pairs={{0,8},{4,28},{8,16},{12,4},{16,24},{20,12},{24,0},{28,20},{1,9},{5... | collective-permute-start | bytes 884744 | tf_op jit(solution)/shard_map/ppermute | solution.py:35
  146.3 3.6 %collective-permute-start.26 = (bf16[144,1024]{1,0:T(8,128)(2,1)S(1)}, bf16[144,1024]{1,0:T(8,128)(2,1)S(1)}, u32[]{:S(2)}, u32[]{:S(2)}) collective-permute-start(bf16[144,1024]{1,0:T(8,128)(2,1)S(1)} %get-tuple-element.84), channel_id=1, source_target_pairs={{0,24},{4,12},{8,0},{12,20},{16,8},{20,28},{24,16},{28,4},{1,25},{... | collective-permute-start | bytes 884744 | tf_op jit(solution)/shard_map/ppermute | solution.py:35
  150.8 2.1 %collective-permute-start.27 = (f32[16,1024]{1,0:T(8,128)S(1)}, f32[16,1024]{1,0:T(8,128)S(1)}, u32[]{:S(2)}, u32[]{:S(2)}) collective-permute-start(f32[16,1024]{1,0:T(8,128)S(1)} %add_multiply_fusion.3), channel_id=1, source_target_pairs={{0,64},{4,68},{32,96},{36,100},{64,0},{68,4},{96,32},{100,36},{1,6... | collective-permute-start | bytes 196616 | tf_op jit(solution)/shard_map/ppermute | solution.py:35
  (94 shorter events, 40.4 us)
Async XLA Ops:
  0.7 21.5 %collective-permute-start.2 = (bf16[128,4096]{1,0:T(8,128)(2,1)}, bf16[128,4096]{1,0:T(8,128)(2,1)}, u32[]{:S(2)}, u32[]{:S(2)}) collective-permute-start(bf16[128,4096]{1,0:T(8,128)(2,1)} %refs_0_.1), channel_id=1, source_target_pairs={{0,32},{4,100},{32,64},{36,4},{64,96},{68,36},{96,0},{100,68},{1,3... | collective-permute-start | bytes 3145736 | tf_op jit(solution)/shard_map/ppermute | solution.py:35
  4.2 26.2 %collective-permute-start = (bf16[544,1024]{1,0:T(8,128)(2,1)S(1)}, bf16[544,1024]{1,0:T(8,128)(2,1)S(1)}, u32[]{:S(2)}, u32[]{:S(2)}) collective-permute-start(bf16[544,1024]{1,0:T(8,128)(2,1)S(1)} %fusion.2.refs_0_), channel_id=1, source_target_pairs={{0,1},{4,7},{1,2},{5,4},{2,3},{6,5},{3,0},{7,6},{8,9},{12,15},{9,1... | collective-permute-start | bytes 3342344 | tf_op jit(solution)/shard_map/ppermute | solution.py:35
  5.7 26.2 %collective-permute-start.1 = (bf16[544,1024]{1,0:T(8,128)(2,1)S(1)}, bf16[544,1024]{1,0:T(8,128)(2,1)}, u32[]{:S(2)}, u32[]{:S(2)}) collective-permute-start(bf16[544,1024]{1,0:T(8,128)(2,1)S(1)} %fusion.2.refs_0_), channel_id=1, source_target_pairs={{0,3},{4,5},{1,0},{5,6},{2,1},{6,7},{3,2},{7,4},{8,11},{12,13},{9,... | collective-permute-start | bytes 3342344 | tf_op jit(solution)/shard_map/ppermute | solution.py:35
  7.5 24.5 %collective-permute-start.4 = (bf16[544,1024]{1,0:T(8,128)(2,1)S(1)}, bf16[544,1024]{1,0:T(8,128)(2,1)}, u32[]{:S(2)}, u32[]{:S(2)}) collective-permute-start(bf16[544,1024]{1,0:T(8,128)(2,1)S(1)} %fusion.2.refs_0_), channel_id=1, source_target_pairs={{0,4},{4,0},{1,5},{5,1},{2,6},{6,2},{3,7},{7,3},{8,12},{12,8},{9,1... | collective-permute-start | bytes 3342344 | tf_op jit(solution)/shard_map/ppermute | solution.py:22
  7.7 18.8 %collective-permute-start.3 = (bf16[128,4096]{1,0:T(8,128)(2,1)S(1)}, bf16[128,4096]{1,0:T(8,128)(2,1)}, u32[]{:S(2)}, u32[]{:S(2)}) collective-permute-start(bf16[128,4096]{1,0:T(8,128)(2,1)S(1)} %copy-done.2), channel_id=1, source_target_pairs={{0,96},{4,36},{32,0},{36,68},{64,32},{68,100},{96,64},{100,4},{1,9... | collective-permute-start | bytes 3145736 | tf_op jit(solution)/shard_map/ppermute | solution.py:35
  32.8 19.8 %collective-permute-start.6 = (bf16[544,1024]{1,0:T(8,128)(2,1)S(1)}, bf16[544,1024]{1,0:T(8,128)(2,1)}, u32[]{:S(2)}, u32[]{:S(2)}) collective-permute-start(bf16[544,1024]{1,0:T(8,128)(2,1)S(1)} %collective-permute-done.refs_3_), channel_id=1, source_target_pairs={{0,1},{4,7},{1,2},{5,4},{2,3},{6,5},{3,0},{7,6},{8,9},{12,15},{9,1... | collective-permute-start | bytes 3342344 | tf_op jit(solution)/shard_map/ppermute | solution.py:35
  33.4 19.3 %collective-permute-start.8 = (bf16[544,1024]{1,0:T(8,128)(2,1)S(1)}, bf16[544,1024]{1,0:T(8,128)(2,1)S(1)}, u32[]{:S(2)}, u32[]{:S(2)}) collective-permute-start(bf16[544,1024]{1,0:T(8,128)(2,1)S(1)} %collective-permute-done.refs_3_), channel_id=1, source_target_pairs={{0,4},{4,0},{1,5},{5,1},{2,6},{6,2},{3,7},{7,3},{8,12},{12,8},{9,1... | collective-permute-start | bytes 3342344 | tf_op jit(solution)/shard_map/ppermute | solution.py:22
  36.0 16.7 %collective-permute-start.9 = (bf16[544,1024]{1,0:T(8,128)(2,1)}, bf16[544,1024]{1,0:T(8,128)(2,1)}, u32[]{:S(2)}, u32[]{:S(2)}) collective-permute-start(bf16[544,1024]{1,0:T(8,128)(2,1)} %collective-permute-done.1.refs_1_), channel_id=1, source_target_pairs={{0,4},{4,0},{1,5},{5,1},{2,6},{6,2},{3,7},{7,3},{8,12},{12,8},{9,1... | collective-permute-start | bytes 3342344 | tf_op jit(solution)/shard_map/ppermute | solution.py:22
  36.0 16.6 %collective-permute-start.7 = (bf16[128,4096]{1,0:T(8,128)(2,1)}, bf16[128,4096]{1,0:T(8,128)(2,1)}, u32[]{:S(2)}, u32[]{:S(2)}) collective-permute-start(bf16[128,4096]{1,0:T(8,128)(2,1)} %collective-permute-done.2.refs_2_), channel_id=1, source_target_pairs={{0,32},{4,100},{32,64},{36,4},{64,96},{68,36},{96,0},{100,68},{1,3... | collective-permute-start | bytes 3145736 | tf_op jit(solution)/shard_map/ppermute | solution.py:35
  36.0 16.6 %collective-permute-start.11 = (bf16[128,4096]{1,0:T(8,128)(2,1)}, bf16[128,4096]{1,0:T(8,128)(2,1)}, u32[]{:S(2)}, u32[]{:S(2)}) collective-permute-start(bf16[128,4096]{1,0:T(8,128)(2,1)} %collective-permute-done.3.refs_1_), channel_id=1, source_target_pairs={{0,4},{4,0},{1,5},{5,1},{2,6},{6,2},{3,7},{7,3},{8,12},{12,8},{9,1... | collective-permute-start | bytes 3145736 | tf_op jit(solution)/shard_map/ppermute | solution.py:22
  47.7 54.2 %all-to-all-start = ((bf16[4,128,4096]{2,1,0:T(8,128)(2,1)}), bf16[4,128,4096]{2,1,0:T(8,128)(2,1)}, u32[]{:S(2)}, u32[]{:S(2)}) async-start(bf16[4,128,4096]{2,1,0:T(8,128)(2,1)} %bitcast.7), calls=%async_computation | async-start | bytes 8388608 | tf_op jit(solution)/shard_map/all_to_all | solution.py:320
  52.8 19.0 %collective-permute-start.16 = (bf16[128,4096]{1,0:T(8,128)(2,1)}, bf16[128,4096]{1,0:T(8,128)(2,1)S(1)}, u32[]{:S(2)}, u32[]{:S(2)}) collective-permute-start(bf16[128,4096]{1,0:T(8,128)(2,1)} %collective-permute-done.7.refs_3_), channel_id=1, source_target_pairs={{0,4},{4,0},{1,5},{5,1},{2,6},{6,2},{3,7},{7,3},{8,12},{12,8},{9,1... | collective-permute-start | bytes 3145736 | tf_op jit(solution)/shard_map/ppermute | solution.py:22
  70.5 18.7 %collective-permute-start.14 = (bf16[528,1024]{1,0:T(8,128)(2,1)}, bf16[528,1024]{1,0:T(8,128)(2,1)}, u32[]{:S(2)}, u32[]{:S(2)}) collective-permute-start(bf16[528,1024]{1,0:T(8,128)(2,1)} %get-tuple-element.58), channel_id=1, source_target_pairs={{0,32},{4,100},{32,64},{36,4},{64,96},{68,36},{96,0},{100,68},{1,3... | collective-permute-start | bytes 3244040 | tf_op jit(solution)/shard_map/ppermute | solution.py:35
  82.8 27.9 %collective-permute-start.17 = (bf16[144,4096]{1,0:T(8,128)(2,1)}, bf16[144,4096]{1,0:T(8,128)(2,1)S(1)}, u32[]{:S(2)}, u32[]{:S(2)}) collective-permute-start(bf16[144,4096]{1,0:T(8,128)(2,1)} %get-tuple-element.70), channel_id=1, source_target_pairs={{0,8},{4,28},{8,16},{12,4},{16,24},{20,12},{24,0},{28,20},{1,9},{5... | collective-permute-start | bytes 3538952 | tf_op jit(solution)/shard_map/ppermute | solution.py:35
  84.8 28.7 %collective-permute-start.18 = (bf16[144,4096]{1,0:T(8,128)(2,1)}, bf16[144,4096]{1,0:T(8,128)(2,1)S(1)}, u32[]{:S(2)}, u32[]{:S(2)}) collective-permute-start(bf16[144,4096]{1,0:T(8,128)(2,1)} %get-tuple-element.71), channel_id=1, source_target_pairs={{0,24},{4,12},{8,0},{12,20},{16,8},{20,28},{24,16},{28,4},{1,25},{... | collective-permute-start | bytes 3538952 | tf_op jit(solution)/shard_map/ppermute | solution.py:35
  87.0 15.5 %collective-permute-start.15 = (bf16[528,1024]{1,0:T(8,128)(2,1)}, bf16[528,1024]{1,0:T(8,128)(2,1)}, u32[]{:S(2)}, u32[]{:S(2)}) collective-permute-start(bf16[528,1024]{1,0:T(8,128)(2,1)} %get-tuple-element.59), channel_id=1, source_target_pairs={{0,96},{4,36},{32,0},{36,68},{64,32},{68,100},{96,64},{100,4},{1,9... | collective-permute-start | bytes 3244040 | tf_op jit(solution)/shard_map/ppermute | solution.py:35
  113.5 16.6 %collective-permute-start.20 = (bf16[528,1024]{1,0:T(8,128)(2,1)}, bf16[528,1024]{1,0:T(8,128)(2,1)S(1)}, u32[]{:S(2)}, u32[]{:S(2)}) collective-permute-start(bf16[528,1024]{1,0:T(8,128)(2,1)} %pad_maximum_fusion.1), channel_id=1, source_target_pairs={{0,32},{4,100},{32,64},{36,4},{64,96},{68,36},{96,0},{100,68},{1,3... | collective-permute-start | bytes 3244040 | tf_op jit(solution)/shard_map/ppermute | solution.py:35
  115.1 17.8 %collective-permute-start.19 = (bf16[144,4096]{1,0:T(8,128)(2,1)S(1)}, bf16[144,4096]{1,0:T(8,128)(2,1)S(1)}, u32[]{:S(2)}, u32[]{:S(2)}) collective-permute-start(bf16[144,4096]{1,0:T(8,128)(2,1)S(1)} %pad_maximum_fusion), channel_id=1, source_target_pairs={{0,8},{4,28},{8,16},{12,4},{16,24},{20,12},{24,0},{28,20},{1,9},{5... | collective-permute-start | bytes 3538952 | tf_op jit(solution)/shard_map/ppermute | solution.py:35
  134.8 11.5 %collective-permute-start.21 = (bf16[144,1024]{1,0:T(8,128)(2,1)S(1)}, bf16[144,1024]{1,0:T(8,128)(2,1)S(1)}, u32[]{:S(2)}, u32[]{:S(2)}) collective-permute-start(bf16[144,1024]{1,0:T(8,128)(2,1)S(1)} %get-tuple-element.86), channel_id=1, source_target_pairs={{0,2},{4,6},{1,3},{5,7},{2,0},{6,4},{3,1},{7,5},{8,10},{12,14},{9,... | collective-permute-start | bytes 884744 | tf_op jit(solution)/shard_map/ppermute | solution.py:35
  138.4 12.1 %collective-permute-start.22 = (bf16[144,1024]{1,0:T(8,128)(2,1)S(1)}, bf16[144,1024]{1,0:T(8,128)(2,1)S(1)}, u32[]{:S(2)}, u32[]{:S(2)}) collective-permute-start(bf16[144,1024]{1,0:T(8,128)(2,1)S(1)} %get-tuple-element.87), channel_id=1, source_target_pairs={{0,1},{4,7},{1,2},{5,4},{2,3},{6,5},{3,0},{7,6},{8,9},{12,15},{9,1... | collective-permute-start | bytes 884744 | tf_op jit(solution)/shard_map/ppermute | solution.py:35
  138.9 11.9 %collective-permute-start.23 = (bf16[144,1024]{1,0:T(8,128)(2,1)S(1)}, bf16[144,1024]{1,0:T(8,128)(2,1)S(1)}, u32[]{:S(2)}, u32[]{:S(2)}) collective-permute-start(bf16[144,1024]{1,0:T(8,128)(2,1)S(1)} %get-tuple-element.88), channel_id=1, source_target_pairs={{0,3},{4,5},{1,0},{5,6},{2,1},{6,7},{3,2},{7,4},{8,11},{12,13},{9,... | collective-permute-start | bytes 884744 | tf_op jit(solution)/shard_map/ppermute | solution.py:35
  141.6 14.2 %collective-permute-start.24 = (bf16[144,1024]{1,0:T(8,128)(2,1)S(1)}, bf16[144,1024]{1,0:T(8,128)(2,1)S(1)}, u32[]{:S(2)}, u32[]{:S(2)}) collective-permute-start(bf16[144,1024]{1,0:T(8,128)(2,1)S(1)} %get-tuple-element.82), channel_id=1, source_target_pairs={{0,16},{4,20},{8,24},{12,28},{16,0},{20,4},{24,8},{28,12},{1,17},{... | collective-permute-start | bytes 884744 | tf_op jit(solution)/shard_map/ppermute | solution.py:35
  143.8 13.3 %collective-permute-start.25 = (bf16[144,1024]{1,0:T(8,128)(2,1)S(1)}, bf16[144,1024]{1,0:T(8,128)(2,1)S(1)}, u32[]{:S(2)}, u32[]{:S(2)}) collective-permute-start(bf16[144,1024]{1,0:T(8,128)(2,1)S(1)} %get-tuple-element.83), channel_id=1, source_target_pairs={{0,8},{4,28},{8,16},{12,4},{16,24},{20,12},{24,0},{28,20},{1,9},{5... | collective-permute-start | bytes 884744 | tf_op jit(solution)/shard_map/ppermute | solution.py:35
  146.3 10.8 %collective-permute-start.26 = (bf16[144,1024]{1,0:T(8,128)(2,1)S(1)}, bf16[144,1024]{1,0:T(8,128)(2,1)S(1)}, u32[]{:S(2)}, u32[]{:S(2)}) collective-permute-start(bf16[144,1024]{1,0:T(8,128)(2,1)S(1)} %get-tuple-element.84), channel_id=1, source_target_pairs={{0,24},{4,12},{8,0},{12,20},{16,8},{20,28},{24,16},{28,4},{1,25},{... | collective-permute-start | bytes 884744 | tf_op jit(solution)/shard_map/ppermute | solution.py:35
  (20 other events, 141.9 us)

commit v2 on v1

--- a/solution.py
+++ b/solution.py
@@ -70,7 +70,7 @@
     out[...] = mm(left[...], right[...]).astype(bf16)
 
 
-def share_product(left, right, tile=512):
+def share_product(left, right, tile=1024):
     return pl.pallas_call(
         share_kernel,
         grid=(right.shape[1] // tile,),
@@ -250,7 +250,7 @@
         copy.wait()
 
 
-def activation_pieces(pieces, extra, numbers, tile=512):
+def activation_pieces(pieces, extra, numbers, tile=1024):
     count, width = len(pieces), pieces[0].shape[1]
     tokens = sum(piece.shape[0] for piece in pieces)
     rank = extra[0].shape[0]
@@ -325,7 +325,7 @@
     grad_far, grad_back = travel(grad[2], "y", 1), travel(grad[3], "y", -1)
     act_far, act_back = travel(act[2], "z", 1), travel(act[3], "z", -1)
     grad_next = pass_on(grad[1], grad_far, ring * lane)
-    grad_next, grad_back, act_far, act_back, shares = together(grad_next, grad_back, act_far, act_back, shares)
+    grad_back, act_far, act_back, shares = together(grad_back, act_far, act_back, shares)
     grad_front = travel(grad_next, "y", 1)
     act_front = travel(pass_on(act[1], act_far, lane), "z", 1)
     input_gradient = (tn(delta, down) + jnp.sum(shares.astype(f32), 0)).astype(bf16)

time: 161 us -> 158 us (0.981)
  starting transfers between devices: 46.8 us -> 42.5 us
  waiting for transfers between devices: 55.1 us -> 58.5 us
    ppermute x21, waiting for transfers between devices: 44.6 us -> 49.4 us  [travel(): return lax.ppermute(array, order, pairs)]
    ppermute x21, starting transfers between devices: 36.2 us -> 31.9 us  [travel(): return lax.ppermute(array, order, pairs)]
    pallas_call x1, Pallas kernels: 10.4 us -> 8.83 us  [share_product(): pl.pallas_call(share_kernel, grid=(right.shape[1] // tile,), in_specs=[pl...]
  transfers between devices with their start and end apart: 31 -> 31, of which waited for: 14 -> 14; matrix products, arithmetic and copies ran while one was open for 11% -> 12% of each run, Pallas kernels for 22% -> 21%
where the time goes in v2:
time: 158 us; the launch traced here: 157 us
  waiting for transfers between devices  58.5 us (37%)
  starting transfers between devices  42.5 us (27%)
  Pallas kernels  33.5 us (21%)
  other arithmetic  16 us (10%)
  matrix products  3.05 us (2%)
  local copies, waits for them, and re-layouts  2.92 us (2%)
    ppermute x21, waiting for transfers between devices, travel(): return lax.ppermute(array, order, pairs)  49.4 us
    ppermute x21, starting transfers between devices, travel(): return lax.ppermute(array, order, pairs)  31.9 us
    pallas_call x1, Pallas kernels, gradient_pieces(): pl.pallas_call(gradient_kernel, grid_spec=pltpu.PrefetchScalarGridSpec(nu...  10.5 us
    pallas_call x1, Pallas kernels, activation_pieces(): pl.pallas_call(functools.partial(activation_kernel, tile), grid_spec=pltp...  10.1 us
    pallas_call x1, Pallas kernels, share_product(): pl.pallas_call(share_kernel, grid=(right.shape[1] // tile,), in_specs=[pl...  8.83 us
    all_to_all x1, waiting for transfers between devices, per_device(): shares = lax.all_to_all(share, 'x', 0, 0)  7.55 us
    ppermute x9, starting transfers between devices, shift(): lax.ppermute(array, axis, [(i, (i + step) % size) for i in range(size)])  5.72 us
    all_to_all x1, starting transfers between devices, per_device(): shares = lax.all_to_all(share, 'x', 0, 0)  4.87 us
  transfers between devices with their start and end apart: 31, of which 14 were waited for; matrix products, arithmetic and copies ran while one was open for 12% of the time, Pallas kernels for 21%

profile of v2, /device:TPU:0, one launch (start us, length us, event | category | flops | bytes accessed | tf_op | source)
XLA Modules:
  0.0 157.4 jit_solution(13707564285955732383)
XLA Ops:
  7.7 2.0 %collective-permute-start.3 = (bf16[128,4096]{1,0:T(8,128)(2,1)S(1)}, bf16[128,4096]{1,0:T(8,128)(2,1)}, u32[]{:S(2)}, u32[]{:S(2)}) collective-permute-start(bf16[128,4096]{1,0:T(8,128)(2,1)S(1)} %copy-done.2), channel_id=1, source_target_pairs={{0,96},{4,36},{32,0},{36,68},{64,32},{68,100},{96,64},{100,4},{1,9... | collective-permute-start | bytes 3145736 | tf_op jit(solution)/shard_map/ppermute | solution.py:35
  9.7 12.5 %collective-permute-done.2.refs_2_ = bf16[128,4096]{1,0:T(8,128)(2,1)} collective-permute-done((bf16[128,4096]{1,0:T(8,128)(2,1)}, bf16[128,4096]{1,0:T(8,128)(2,1)}, u32[]{:S(2)}, u32[]{:S(2)}) %collective-permute-start.2) | collective-permute-done | bytes 1048608 | tf_op jit(solution)/shard_map/ppermute | solution.py:35
  23.4 3.1 %collective-permute-done.3.refs_1_ = bf16[128,4096]{1,0:T(8,128)(2,1)} collective-permute-done((bf16[128,4096]{1,0:T(8,128)(2,1)S(1)}, bf16[128,4096]{1,0:T(8,128)(2,1)}, u32[]{:S(2)}, u32[]{:S(2)}) %collective-permute-start.3) | collective-permute-done | bytes 1048608 | tf_op jit(solution)/shard_map/ppermute | solution.py:35
  26.5 3.8 %collective-permute-done.refs_3_ = bf16[544,1024]{1,0:T(8,128)(2,1)S(1)} collective-permute-done((bf16[544,1024]{1,0:T(8,128)(2,1)S(1)}, bf16[544,1024]{1,0:T(8,128)(2,1)S(1)}, u32[]{:S(2)}, u32[]{:S(2)}) %collective-permute-start) | collective-permute-done | bytes 1114144 | tf_op jit(solution)/shard_map/ppermute | solution.py:35
  33.4 2.6 %collective-permute-start.8 = (bf16[544,1024]{1,0:T(8,128)(2,1)S(1)}, bf16[544,1024]{1,0:T(8,128)(2,1)S(1)}, u32[]{:S(2)}, u32[]{:S(2)}) collective-permute-start(bf16[544,1024]{1,0:T(8,128)(2,1)S(1)} %collective-permute-done.refs_3_), channel_id=1, source_target_pairs={{0,4},{4,0},{1,5},{5,1},{2,6},{6,2},{3,7},{7,3},{8,12},{12,8},{9,1... | collective-permute-start | bytes 3342344 | tf_op jit(solution)/shard_map/ppermute | solution.py:22
  37.3 8.8 %shard_map.92 = bf16[512,4096]{1,0:T(8,128)(2,1)} custom-call(bf16[512,1024]{1,0:T(8,128)(2,1)} %left.1, bf16[1024,4096]{1,0:T(8,128)(2,1)} %right.1), custom_call_target="tpu_custom_call" | custom-call | flops 4294967296 | bytes 8388608 | tf_op jit(solution)/shard_map/pallas_call | solution.py:74
  46.1 4.9 %all-to-all-start = ((bf16[4,128,4096]{2,1,0:T(8,128)(2,1)}), bf16[4,128,4096]{2,1,0:T(8,128)(2,1)}, u32[]{:S(2)}, u32[]{:S(2)}) async-start(bf16[4,128,4096]{2,1,0:T(8,128)(2,1)} %bitcast.7), calls=%async_computation | async-start | bytes 8388608 | tf_op jit(solution)/shard_map/all_to_all | solution.py:320
  52.9 4.1 %shard_map.93 = (bf16[16,4096]{1,0:T(8,128)(2,1)}, bf16[16,128]{1,0:T(8,128)(2,1)}) custom-call(s32[1]{0:T(128)} %bitcast.place, bf16[544,1024]{1,0:T(8,128)(2,1)} %copy-done.1, bf16[544,1024]{1,0:T(8,128)(2,1)} %collective-permute-done.1.refs_1_, bf16[544,1024]{1,0:T(8,128)(2,1)} %collective-permute-done.6.refs_2_, bf16[544,1024]{1,0:T(8,128)(2,1)} %copy-done.3, ...), custom_call_target="tpu_custom_call" | custom-call | flops 1024 | bytes 1024 | tf_op jit(solution)/shard_map/pallas_call | solution.py:111
  59.7 10.5 %shard_map.94 = (bf16[528,1024]{1,0:T(8,128)(2,1)}, bf16[528,1024]{1,0:T(8,128)(2,1)}, bf16[528,1024]{1,0:T(8,128)(2,1)}, bf16[528,1024]{1,0:T(8,128)(2,1)}) custom-call(s32[13]{0:T(128)} %pad_add_fusion.numbers, bf16[544,1024]{1,0:T(8,128)(2,1)} %copy-done.1, bf16[544,1024]{1,0:T(8,128)(2,1)} %collective-permute-done.1.refs_1_, ...), custom_call_target="tpu_custom_call" | custom-call | flops 1024 | bytes 1024 | tf_op jit(solution)/shard_map/pallas_call | solution.py:201
  71.5 10.1 %shard_map.95 = (bf16[144,4096]{1,0:T(8,128)(2,1)}, bf16[144,4096]{1,0:T(8,128)(2,1)}, bf16[144,4096]{1,0:T(8,128)(2,1)}, bf16[144,4096]{1,0:T(8,128)(2,1)}) custom-call(s32[4]{0:T(128)} %fusion.14.numbers, bf16[128,4096]{1,0:T(8,128)(2,1)} %refs_0_.1, bf16[128,4096]{1,0:T(8,128)(2,1)} %collective-permute-done.3.refs_1_, ...), custom_call_target="tpu_custom_call" | custom-call | flops 1024 | bytes 1024 | tf_op jit(solution)/shard_map/pallas_call | solution.py:257
  81.6 2.0 %collective-permute-start.16 = (bf16[144,4096]{1,0:T(8,128)(2,1)}, bf16[144,4096]{1,0:T(8,128)(2,1)S(1)}, u32[]{:S(2)}, u32[]{:S(2)}) collective-permute-start(bf16[144,4096]{1,0:T(8,128)(2,1)} %get-tuple-element.67), channel_id=1, source_target_pairs={{0,8},{4,28},{8,16},{12,4},{16,24},{20,12},{24,0},{28,20},{1,9},{5... | collective-permute-start | bytes 3538952 | tf_op jit(solution)/shard_map/ppermute | solution.py:35
  83.6 2.2 %collective-permute-start.17 = (bf16[144,4096]{1,0:T(8,128)(2,1)}, bf16[144,4096]{1,0:T(8,128)(2,1)S(1)}, u32[]{:S(2)}, u32[]{:S(2)}) collective-permute-start(bf16[144,4096]{1,0:T(8,128)(2,1)} %get-tuple-element.68), channel_id=1, source_target_pairs={{0,24},{4,12},{8,0},{12,20},{16,8},{20,28},{24,16},{28,4},{1,25},{... | collective-permute-start | bytes 3538952 | tf_op jit(solution)/shard_map/ppermute | solution.py:35
  85.8 3.2 %collective-permute-start.14 = (bf16[528,1024]{1,0:T(8,128)(2,1)}, bf16[528,1024]{1,0:T(8,128)(2,1)}, u32[]{:S(2)}, u32[]{:S(2)}) collective-permute-start(bf16[528,1024]{1,0:T(8,128)(2,1)} %get-tuple-element.56), channel_id=1, source_target_pairs={{0,96},{4,36},{32,0},{36,68},{64,32},{68,100},{96,64},{100,4},{1,9... | collective-permute-start | bytes 3244040 | tf_op jit(solution)/shard_map/ppermute | solution.py:35
  89.8 1.9 %add_convert_fusion = bf16[512,1024]{1,0:T(8,128)(2,1)S(1)} fusion(bf16[528,1024]{1,0:T(8,128)(2,1)} %collective-permute-done.19, bf16[528,1024]{1,0:T(8,128)(2,1)} %get-tuple-element.72), kind=kLoop, calls=%fused_computation.15 | loop fusion | flops 2097152 | bytes 3145728 | tf_op jit(solution)/shard_map/convert_element_type | solution.py:323
  92.8 7.5 %all-to-all-done = bf16[4,128,4096]{2,1,0:T(8,128)(2,1)} async-done(((bf16[4,128,4096]{2,1,0:T(8,128)(2,1)}), bf16[4,128,4096]{2,1,0:T(8,128)(2,1)}, u32[]{:S(2)}, u32[]{:S(2)}) %all-to-all-start) | async-done | bytes 4194336 | tf_op jit(solution)/shard_map/all_to_all | solution.py:320
  100.3 10.1 %collective-permute-done.14 = bf16[528,1024]{1,0:T(8,128)(2,1)} collective-permute-done((bf16[528,1024]{1,0:T(8,128)(2,1)}, bf16[528,1024]{1,0:T(8,128)(2,1)}, u32[]{:S(2)}, u32[]{:S(2)}) %collective-permute-start.14) | collective-permute-done | bytes 1081376 | tf_op jit(solution)/shard_map/ppermute | solution.py:35
  114.4 3.2 %convert_reduce_fusion = f32[128,4096]{1,0:T(8,128)S(1)} fusion(bf16[4,128,4096]{2,1,0:T(8,128)(2,1)} %all-to-all-done), kind=kLoop, calls=%fused_computation | loop fusion | flops 3670016 | bytes 6291456 | tf_op jit(solution)/shard_map/reduce_sum | solution.py:331
  119.1 2.2 %add_add_fusion.1 = bf16[512,1024]{1,0:T(8,128)(2,1)S(1)} fusion(bf16[528,1024]{1,0:T(8,128)(2,1)} %collective-permute-done.20, bf16[528,1024]{1,0:T(8,128)(2,1)} %collective-permute-done.14, bf16[528,1024]{1,0:T(8,128)(2,1)S(1)} %copy-done.7), kind=kLoop, calls=%fused_computation.14 | loop fusion | flops 3145728 | bytes 4194304 | tf_op jit(solution)/shard_map/add | solution.py:336
  122.3 9.4 %collective-permute-done.18 = bf16[144,4096]{1,0:T(8,128)(2,1)S(1)} collective-permute-done((bf16[144,4096]{1,0:T(8,128)(2,1)S(1)}, bf16[144,4096]{1,0:T(8,128)(2,1)S(1)}, u32[]{:S(2)}, u32[]{:S(2)}) %collective-permute-start.18) | collective-permute-done | bytes 1179680 | tf_op jit(solution)/shard_map/ppermute | solution.py:35
  132.4 3.3 %collective-permute-start.21 = (bf16[144,1024]{1,0:T(8,128)(2,1)S(1)}, bf16[144,1024]{1,0:T(8,128)(2,1)S(1)}, u32[]{:S(2)}, u32[]{:S(2)}) collective-permute-start(bf16[144,1024]{1,0:T(8,128)(2,1)S(1)} %get-tuple-element.84), channel_id=1, source_target_pairs={{0,2},{4,6},{1,3},{5,7},{2,0},{6,4},{3,1},{7,5},{8,10},{12,14},{9,... | collective-permute-start | bytes 884744 | tf_op jit(solution)/shard_map/ppermute | solution.py:35
  136.2 2.7 %collective-permute-start.23 = (bf16[144,1024]{1,0:T(8,128)(2,1)S(1)}, bf16[144,1024]{1,0:T(8,128)(2,1)S(1)}, u32[]{:S(2)}, u32[]{:S(2)}) collective-permute-start(bf16[144,1024]{1,0:T(8,128)(2,1)S(1)} %get-tuple-element.86), channel_id=1, source_target_pairs={{0,3},{4,5},{1,0},{5,6},{2,1},{6,7},{3,2},{7,4},{8,11},{12,13},{9,... | collective-permute-start | bytes 884744 | tf_op jit(solution)/shard_map/ppermute | solution.py:35
  141.8 2.2 %collective-permute-done.21 = bf16[144,1024]{1,0:T(8,128)(2,1)S(1)} collective-permute-done((bf16[144,1024]{1,0:T(8,128)(2,1)S(1)}, bf16[144,1024]{1,0:T(8,128)(2,1)S(1)}, u32[]{:S(2)}, u32[]{:S(2)}) %collective-permute-start.21) | collective-permute-done | bytes 294944 | tf_op jit(solution)/shard_map/ppermute | solution.py:35
  144.0 2.0 %collective-permute-start.26 = (bf16[144,1024]{1,0:T(8,128)(2,1)S(1)}, bf16[144,1024]{1,0:T(8,128)(2,1)S(1)}, u32[]{:S(2)}, u32[]{:S(2)}) collective-permute-start(bf16[144,1024]{1,0:T(8,128)(2,1)S(1)} %get-tuple-element.82), channel_id=1, source_target_pairs={{0,24},{4,12},{8,0},{12,20},{16,8},{20,28},{24,16},{28,4},{1,25},{... | collective-permute-start | bytes 884744 | tf_op jit(solution)/shard_map/ppermute | solution.py:35
  145.9 2.1 %collective-permute-done.22 = bf16[144,1024]{1,0:T(8,128)(2,1)S(1)} collective-permute-done((bf16[144,1024]{1,0:T(8,128)(2,1)S(1)}, bf16[144,1024]{1,0:T(8,128)(2,1)S(1)}, u32[]{:S(2)}, u32[]{:S(2)}) %collective-permute-start.22) | collective-permute-done | bytes 294944 | tf_op jit(solution)/shard_map/ppermute | solution.py:35
  (94 shorter events, 40.1 us)
Async XLA Ops:
  0.7 21.5 %collective-permute-start.2 = (bf16[128,4096]{1,0:T(8,128)(2,1)}, bf16[128,4096]{1,0:T(8,128)(2,1)}, u32[]{:S(2)}, u32[]{:S(2)}) collective-permute-start(bf16[128,4096]{1,0:T(8,128)(2,1)} %refs_0_.1), channel_id=1, source_target_pairs={{0,32},{4,100},{32,64},{36,4},{64,96},{68,36},{96,0},{100,68},{1,3... | collective-permute-start | bytes 3145736 | tf_op jit(solution)/shard_map/ppermute | solution.py:35
  4.2 26.2 %collective-permute-start = (bf16[544,1024]{1,0:T(8,128)(2,1)S(1)}, bf16[544,1024]{1,0:T(8,128)(2,1)S(1)}, u32[]{:S(2)}, u32[]{:S(2)}) collective-permute-start(bf16[544,1024]{1,0:T(8,128)(2,1)S(1)} %fusion.2.refs_0_), channel_id=1, source_target_pairs={{0,1},{4,7},{1,2},{5,4},{2,3},{6,5},{3,0},{7,6},{8,9},{12,15},{9,1... | collective-permute-start | bytes 3342344 | tf_op jit(solution)/shard_map/ppermute | solution.py:35
  5.7 26.2 %collective-permute-start.1 = (bf16[544,1024]{1,0:T(8,128)(2,1)S(1)}, bf16[544,1024]{1,0:T(8,128)(2,1)}, u32[]{:S(2)}, u32[]{:S(2)}) collective-permute-start(bf16[544,1024]{1,0:T(8,128)(2,1)S(1)} %fusion.2.refs_0_), channel_id=1, source_target_pairs={{0,3},{4,5},{1,0},{5,6},{2,1},{6,7},{3,2},{7,4},{8,11},{12,13},{9,... | collective-permute-start | bytes 3342344 | tf_op jit(solution)/shard_map/ppermute | solution.py:35
  7.5 24.5 %collective-permute-start.4 = (bf16[544,1024]{1,0:T(8,128)(2,1)S(1)}, bf16[544,1024]{1,0:T(8,128)(2,1)}, u32[]{:S(2)}, u32[]{:S(2)}) collective-permute-start(bf16[544,1024]{1,0:T(8,128)(2,1)S(1)} %fusion.2.refs_0_), channel_id=1, source_target_pairs={{0,4},{4,0},{1,5},{5,1},{2,6},{6,2},{3,7},{7,3},{8,12},{12,8},{9,1... | collective-permute-start | bytes 3342344 | tf_op jit(solution)/shard_map/ppermute | solution.py:22
  7.7 18.8 %collective-permute-start.3 = (bf16[128,4096]{1,0:T(8,128)(2,1)S(1)}, bf16[128,4096]{1,0:T(8,128)(2,1)}, u32[]{:S(2)}, u32[]{:S(2)}) collective-permute-start(bf16[128,4096]{1,0:T(8,128)(2,1)S(1)} %copy-done.2), channel_id=1, source_target_pairs={{0,96},{4,36},{32,0},{36,68},{64,32},{68,100},{96,64},{100,4},{1,9... | collective-permute-start | bytes 3145736 | tf_op jit(solution)/shard_map/ppermute | solution.py:35
  32.8 19.5 %collective-permute-start.6 = (bf16[544,1024]{1,0:T(8,128)(2,1)S(1)}, bf16[544,1024]{1,0:T(8,128)(2,1)}, u32[]{:S(2)}, u32[]{:S(2)}) collective-permute-start(bf16[544,1024]{1,0:T(8,128)(2,1)S(1)} %collective-permute-done.refs_3_), channel_id=1, source_target_pairs={{0,1},{4,7},{1,2},{5,4},{2,3},{6,5},{3,0},{7,6},{8,9},{12,15},{9,1... | collective-permute-start | bytes 3342344 | tf_op jit(solution)/shard_map/ppermute | solution.py:35
  33.4 19.0 %collective-permute-start.8 = (bf16[544,1024]{1,0:T(8,128)(2,1)S(1)}, bf16[544,1024]{1,0:T(8,128)(2,1)S(1)}, u32[]{:S(2)}, u32[]{:S(2)}) collective-permute-start(bf16[544,1024]{1,0:T(8,128)(2,1)S(1)} %collective-permute-done.refs_3_), channel_id=1, source_target_pairs={{0,4},{4,0},{1,5},{5,1},{2,6},{6,2},{3,7},{7,3},{8,12},{12,8},{9,1... | collective-permute-start | bytes 3342344 | tf_op jit(solution)/shard_map/ppermute | solution.py:22
  36.0 16.4 %collective-permute-start.9 = (bf16[544,1024]{1,0:T(8,128)(2,1)}, bf16[544,1024]{1,0:T(8,128)(2,1)}, u32[]{:S(2)}, u32[]{:S(2)}) collective-permute-start(bf16[544,1024]{1,0:T(8,128)(2,1)} %collective-permute-done.1.refs_1_), channel_id=1, source_target_pairs={{0,4},{4,0},{1,5},{5,1},{2,6},{6,2},{3,7},{7,3},{8,12},{12,8},{9,1... | collective-permute-start | bytes 3342344 | tf_op jit(solution)/shard_map/ppermute | solution.py:22
  36.0 16.3 %collective-permute-start.7 = (bf16[128,4096]{1,0:T(8,128)(2,1)}, bf16[128,4096]{1,0:T(8,128)(2,1)}, u32[]{:S(2)}, u32[]{:S(2)}) collective-permute-start(bf16[128,4096]{1,0:T(8,128)(2,1)} %collective-permute-done.2.refs_2_), channel_id=1, source_target_pairs={{0,32},{4,100},{32,64},{36,4},{64,96},{68,36},{96,0},{100,68},{1,3... | collective-permute-start | bytes 3145736 | tf_op jit(solution)/shard_map/ppermute | solution.py:35
  36.0 16.3 %collective-permute-start.11 = (bf16[128,4096]{1,0:T(8,128)(2,1)}, bf16[128,4096]{1,0:T(8,128)(2,1)}, u32[]{:S(2)}, u32[]{:S(2)}) collective-permute-start(bf16[128,4096]{1,0:T(8,128)(2,1)} %collective-permute-done.3.refs_1_), channel_id=1, source_target_pairs={{0,4},{4,0},{1,5},{5,1},{2,6},{6,2},{3,7},{7,3},{8,12},{12,8},{9,1... | collective-permute-start | bytes 3145736 | tf_op jit(solution)/shard_map/ppermute | solution.py:22
  46.1 54.2 %all-to-all-start = ((bf16[4,128,4096]{2,1,0:T(8,128)(2,1)}), bf16[4,128,4096]{2,1,0:T(8,128)(2,1)}, u32[]{:S(2)}, u32[]{:S(2)}) async-start(bf16[4,128,4096]{2,1,0:T(8,128)(2,1)} %bitcast.7), calls=%async_computation | async-start | bytes 8388608 | tf_op jit(solution)/shard_map/all_to_all | solution.py:320
  52.5 18.0 %collective-permute-start.15 = (bf16[128,4096]{1,0:T(8,128)(2,1)}, bf16[128,4096]{1,0:T(8,128)(2,1)S(1)}, u32[]{:S(2)}, u32[]{:S(2)}) collective-permute-start(bf16[128,4096]{1,0:T(8,128)(2,1)} %collective-permute-done.7.refs_3_), channel_id=1, source_target_pairs={{0,4},{4,0},{1,5},{5,1},{2,6},{6,2},{3,7},{7,3},{8,12},{12,8},{9,1... | collective-permute-start | bytes 3145736 | tf_op jit(solution)/shard_map/ppermute | solution.py:22
  70.2 18.8 %collective-permute-start.19 = (bf16[528,1024]{1,0:T(8,128)(2,1)}, bf16[528,1024]{1,0:T(8,128)(2,1)}, u32[]{:S(2)}, u32[]{:S(2)}) collective-permute-start(bf16[528,1024]{1,0:T(8,128)(2,1)} %get-tuple-element.73), channel_id=1, source_target_pairs={{0,32},{4,100},{32,64},{36,4},{64,96},{68,36},{96,0},{100,68},{1,3... | collective-permute-start | bytes 3244040 | tf_op jit(solution)/shard_map/ppermute | solution.py:35
  81.6 28.8 %collective-permute-start.16 = (bf16[144,4096]{1,0:T(8,128)(2,1)}, bf16[144,4096]{1,0:T(8,128)(2,1)S(1)}, u32[]{:S(2)}, u32[]{:S(2)}) collective-permute-start(bf16[144,4096]{1,0:T(8,128)(2,1)} %get-tuple-element.67), channel_id=1, source_target_pairs={{0,8},{4,28},{8,16},{12,4},{16,24},{20,12},{24,0},{28,20},{1,9},{5... | collective-permute-start | bytes 3538952 | tf_op jit(solution)/shard_map/ppermute | solution.py:35
  83.6 28.7 %collective-permute-start.17 = (bf16[144,4096]{1,0:T(8,128)(2,1)}, bf16[144,4096]{1,0:T(8,128)(2,1)S(1)}, u32[]{:S(2)}, u32[]{:S(2)}) collective-permute-start(bf16[144,4096]{1,0:T(8,128)(2,1)} %get-tuple-element.68), channel_id=1, source_target_pairs={{0,24},{4,12},{8,0},{12,20},{16,8},{20,28},{24,16},{28,4},{1,25},{... | collective-permute-start | bytes 3538952 | tf_op jit(solution)/shard_map/ppermute | solution.py:35
  85.8 24.6 %collective-permute-start.14 = (bf16[528,1024]{1,0:T(8,128)(2,1)}, bf16[528,1024]{1,0:T(8,128)(2,1)}, u32[]{:S(2)}, u32[]{:S(2)}) collective-permute-start(bf16[528,1024]{1,0:T(8,128)(2,1)} %get-tuple-element.56), channel_id=1, source_target_pairs={{0,96},{4,36},{32,0},{36,68},{64,32},{68,100},{96,64},{100,4},{1,9... | collective-permute-start | bytes 3244040 | tf_op jit(solution)/shard_map/ppermute | solution.py:35
  92.8 26.3 %collective-permute-start.20 = (bf16[528,1024]{1,0:T(8,128)(2,1)}, bf16[528,1024]{1,0:T(8,128)(2,1)}, u32[]{:S(2)}, u32[]{:S(2)}) collective-permute-start(bf16[528,1024]{1,0:T(8,128)(2,1)} %pad_maximum_fusion.1), channel_id=1, source_target_pairs={{0,32},{4,100},{32,64},{36,4},{64,96},{68,36},{96,0},{100,68},{1,3... | collective-permute-start | bytes 3244040 | tf_op jit(solution)/shard_map/ppermute | solution.py:35
  113.9 17.8 %collective-permute-start.18 = (bf16[144,4096]{1,0:T(8,128)(2,1)S(1)}, bf16[144,4096]{1,0:T(8,128)(2,1)S(1)}, u32[]{:S(2)}, u32[]{:S(2)}) collective-permute-start(bf16[144,4096]{1,0:T(8,128)(2,1)S(1)} %pad_maximum_fusion), channel_id=1, source_target_pairs={{0,8},{4,28},{8,16},{12,4},{16,24},{20,12},{24,0},{28,20},{1,9},{5... | collective-permute-start | bytes 3538952 | tf_op jit(solution)/shard_map/ppermute | solution.py:35
  132.4 11.5 %collective-permute-start.21 = (bf16[144,1024]{1,0:T(8,128)(2,1)S(1)}, bf16[144,1024]{1,0:T(8,128)(2,1)S(1)}, u32[]{:S(2)}, u32[]{:S(2)}) collective-permute-start(bf16[144,1024]{1,0:T(8,128)(2,1)S(1)} %get-tuple-element.84), channel_id=1, source_target_pairs={{0,2},{4,6},{1,3},{5,7},{2,0},{6,4},{3,1},{7,5},{8,10},{12,14},{9,... | collective-permute-start | bytes 884744 | tf_op jit(solution)/shard_map/ppermute | solution.py:35
  135.7 12.3 %collective-permute-start.22 = (bf16[144,1024]{1,0:T(8,128)(2,1)S(1)}, bf16[144,1024]{1,0:T(8,128)(2,1)S(1)}, u32[]{:S(2)}, u32[]{:S(2)}) collective-permute-start(bf16[144,1024]{1,0:T(8,128)(2,1)S(1)} %get-tuple-element.85), channel_id=1, source_target_pairs={{0,1},{4,7},{1,2},{5,4},{2,3},{6,5},{3,0},{7,6},{8,9},{12,15},{9,1... | collective-permute-start | bytes 884744 | tf_op jit(solution)/shard_map/ppermute | solution.py:35
  136.2 12.0 %collective-permute-start.23 = (bf16[144,1024]{1,0:T(8,128)(2,1)S(1)}, bf16[144,1024]{1,0:T(8,128)(2,1)S(1)}, u32[]{:S(2)}, u32[]{:S(2)}) collective-permute-start(bf16[144,1024]{1,0:T(8,128)(2,1)S(1)} %get-tuple-element.86), channel_id=1, source_target_pairs={{0,3},{4,5},{1,0},{5,6},{2,1},{6,7},{3,2},{7,4},{8,11},{12,13},{9,... | collective-permute-start | bytes 884744 | tf_op jit(solution)/shard_map/ppermute | solution.py:35
  138.9 13.5 %collective-permute-start.24 = (bf16[144,1024]{1,0:T(8,128)(2,1)S(1)}, bf16[144,1024]{1,0:T(8,128)(2,1)S(1)}, u32[]{:S(2)}, u32[]{:S(2)}) collective-permute-start(bf16[144,1024]{1,0:T(8,128)(2,1)S(1)} %get-tuple-element.80), channel_id=1, source_target_pairs={{0,16},{4,20},{8,24},{12,28},{16,0},{20,4},{24,8},{28,12},{1,17},{... | collective-permute-start | bytes 884744 | tf_op jit(solution)/shard_map/ppermute | solution.py:35
  139.9 14.1 %collective-permute-start.25 = (bf16[144,1024]{1,0:T(8,128)(2,1)S(1)}, bf16[144,1024]{1,0:T(8,128)(2,1)S(1)}, u32[]{:S(2)}, u32[]{:S(2)}) collective-permute-start(bf16[144,1024]{1,0:T(8,128)(2,1)S(1)} %get-tuple-element.81), channel_id=1, source_target_pairs={{0,8},{4,28},{8,16},{12,4},{16,24},{20,12},{24,0},{28,20},{1,9},{5... | collective-permute-start | bytes 884744 | tf_op jit(solution)/shard_map/ppermute | solution.py:35
  144.0 10.1 %collective-permute-start.26 = (bf16[144,1024]{1,0:T(8,128)(2,1)S(1)}, bf16[144,1024]{1,0:T(8,128)(2,1)S(1)}, u32[]{:S(2)}, u32[]{:S(2)}) collective-permute-start(bf16[144,1024]{1,0:T(8,128)(2,1)S(1)} %get-tuple-element.82), channel_id=1, source_target_pairs={{0,24},{4,12},{8,0},{12,20},{16,8},{20,28},{24,16},{28,4},{1,25},{... | collective-permute-start | bytes 884744 | tf_op jit(solution)/shard_map/ppermute | solution.py:35
  (20 other events, 136.7 us)

commit v3 on v2

--- a/solution.py
+++ b/solution.py
@@ -325,7 +325,7 @@
     grad_far, grad_back = travel(grad[2], "y", 1), travel(grad[3], "y", -1)
     act_far, act_back = travel(act[2], "z", 1), travel(act[3], "z", -1)
     grad_next = pass_on(grad[1], grad_far, ring * lane)
-    grad_back, act_far, act_back, shares = together(grad_back, act_far, act_back, shares)
+    act_far, act_back, shares = together(act_far, act_back, shares)
     grad_front = travel(grad_next, "y", 1)
     act_front = travel(pass_on(act[1], act_far, lane), "z", 1)
     input_gradient = (tn(delta, down) + jnp.sum(shares.astype(f32), 0)).astype(bf16)

time: 158 us -> 158 us (level)
  no operation moved by 1% of the time
where the time goes in v3:
time: 158 us; the launch traced here: 157 us
  waiting for transfers between devices  58.5 us (37%)
  starting transfers between devices  42.5 us (27%)
  Pallas kernels  33.5 us (21%)
  other arithmetic  16 us (10%)
  matrix products  3.05 us (2%)
  local copies, waits for them, and re-layouts  2.92 us (2%)
    ppermute x21, waiting for transfers between devices, travel(): return lax.ppermute(array, order, pairs)  49.4 us
    ppermute x21, starting transfers between devices, travel(): return lax.ppermute(array, order, pairs)  31.9 us
    pallas_call x1, Pallas kernels, gradient_pieces(): pl.pallas_call(gradient_kernel, grid_spec=pltpu.PrefetchScalarGridSpec(nu...  10.5 us
    pallas_call x1, Pallas kernels, activation_pieces(): pl.pallas_call(functools.partial(activation_kernel, tile), grid_spec=pltp...  10.1 us
    pallas_call x1, Pallas kernels, share_product(): pl.pallas_call(share_kernel, grid=(right.shape[1] // tile,), in_specs=[pl...  8.83 us
    all_to_all x1, waiting for transfers between devices, per_device(): shares = lax.all_to_all(share, 'x', 0, 0)  7.55 us
    ppermute x9, starting transfers between devices, shift(): lax.ppermute(array, axis, [(i, (i + step) % size) for i in range(size)])  5.72 us
    all_to_all x1, starting transfers between devices, per_device(): shares = lax.all_to_all(share, 'x', 0, 0)  4.87 us
  transfers between devices with their start and end apart: 31, of which 14 were waited for; matrix products, arithmetic and copies ran while one was open for 12% of the time, Pallas kernels for 21%

profile of v3, /device:TPU:0, one launch (start us, length us, event | category | flops | bytes accessed | tf_op | source)
XLA Modules:
  0.0 157.4 jit_solution(3778164586060717713)
XLA Ops:
  7.7 2.0 %collective-permute-start.3 = (bf16[128,4096]{1,0:T(8,128)(2,1)S(1)}, bf16[128,4096]{1,0:T(8,128)(2,1)}, u32[]{:S(2)}, u32[]{:S(2)}) collective-permute-start(bf16[128,4096]{1,0:T(8,128)(2,1)S(1)} %copy-done.2), channel_id=1, source_target_pairs={{0,96},{4,36},{32,0},{36,68},{64,32},{68,100},{96,64},{100,4},{1,9... | collective-permute-start | bytes 3145736 | tf_op jit(solution)/shard_map/ppermute | solution.py:35
  9.7 12.5 %collective-permute-done.2.refs_2_ = bf16[128,4096]{1,0:T(8,128)(2,1)} collective-permute-done((bf16[128,4096]{1,0:T(8,128)(2,1)}, bf16[128,4096]{1,0:T(8,128)(2,1)}, u32[]{:S(2)}, u32[]{:S(2)}) %collective-permute-start.2) | collective-permute-done | bytes 1048608 | tf_op jit(solution)/shard_map/ppermute | solution.py:35
  23.4 3.1 %collective-permute-done.3.refs_1_ = bf16[128,4096]{1,0:T(8,128)(2,1)} collective-permute-done((bf16[128,4096]{1,0:T(8,128)(2,1)S(1)}, bf16[128,4096]{1,0:T(8,128)(2,1)}, u32[]{:S(2)}, u32[]{:S(2)}) %collective-permute-start.3) | collective-permute-done | bytes 1048608 | tf_op jit(solution)/shard_map/ppermute | solution.py:35
  26.5 3.8 %collective-permute-done.refs_3_ = bf16[544,1024]{1,0:T(8,128)(2,1)S(1)} collective-permute-done((bf16[544,1024]{1,0:T(8,128)(2,1)S(1)}, bf16[544,1024]{1,0:T(8,128)(2,1)S(1)}, u32[]{:S(2)}, u32[]{:S(2)}) %collective-permute-start) | collective-permute-done | bytes 1114144 | tf_op jit(solution)/shard_map/ppermute | solution.py:35
  33.4 2.6 %collective-permute-start.8 = (bf16[544,1024]{1,0:T(8,128)(2,1)S(1)}, bf16[544,1024]{1,0:T(8,128)(2,1)S(1)}, u32[]{:S(2)}, u32[]{:S(2)}) collective-permute-start(bf16[544,1024]{1,0:T(8,128)(2,1)S(1)} %collective-permute-done.refs_3_), channel_id=1, source_target_pairs={{0,4},{4,0},{1,5},{5,1},{2,6},{6,2},{3,7},{7,3},{8,12},{12,8},{9,1... | collective-permute-start | bytes 3342344 | tf_op jit(solution)/shard_map/ppermute | solution.py:22
  37.3 8.8 %shard_map.92 = bf16[512,4096]{1,0:T(8,128)(2,1)} custom-call(bf16[512,1024]{1,0:T(8,128)(2,1)} %left.1, bf16[1024,4096]{1,0:T(8,128)(2,1)} %right.1), custom_call_target="tpu_custom_call" | custom-call | flops 4294967296 | bytes 8388608 | tf_op jit(solution)/shard_map/pallas_call | solution.py:74
  46.1 4.9 %all-to-all-start = ((bf16[4,128,4096]{2,1,0:T(8,128)(2,1)}), bf16[4,128,4096]{2,1,0:T(8,128)(2,1)}, u32[]{:S(2)}, u32[]{:S(2)}) async-start(bf16[4,128,4096]{2,1,0:T(8,128)(2,1)} %bitcast.7), calls=%async_computation | async-start | bytes 8388608 | tf_op jit(solution)/shard_map/all_to_all | solution.py:320
  52.9 4.1 %shard_map.93 = (bf16[16,4096]{1,0:T(8,128)(2,1)}, bf16[16,128]{1,0:T(8,128)(2,1)}) custom-call(s32[1]{0:T(128)} %bitcast.place, bf16[544,1024]{1,0:T(8,128)(2,1)} %copy-done.1, bf16[544,1024]{1,0:T(8,128)(2,1)} %collective-permute-done.1.refs_1_, bf16[544,1024]{1,0:T(8,128)(2,1)} %collective-permute-done.6.refs_2_, bf16[544,1024]{1,0:T(8,128)(2,1)} %copy-done.3, ...), custom_call_target="tpu_custom_call" | custom-call | flops 1024 | bytes 1024 | tf_op jit(solution)/shard_map/pallas_call | solution.py:111
  59.7 10.5 %shard_map.94 = (bf16[528,1024]{1,0:T(8,128)(2,1)}, bf16[528,1024]{1,0:T(8,128)(2,1)}, bf16[528,1024]{1,0:T(8,128)(2,1)}, bf16[528,1024]{1,0:T(8,128)(2,1)}) custom-call(s32[13]{0:T(128)} %pad_add_fusion.numbers, bf16[544,1024]{1,0:T(8,128)(2,1)} %copy-done.1, bf16[544,1024]{1,0:T(8,128)(2,1)} %collective-permute-done.1.refs_1_, ...), custom_call_target="tpu_custom_call" | custom-call | flops 1024 | bytes 1024 | tf_op jit(solution)/shard_map/pallas_call | solution.py:201
  71.5 10.1 %shard_map.95 = (bf16[144,4096]{1,0:T(8,128)(2,1)}, bf16[144,4096]{1,0:T(8,128)(2,1)}, bf16[144,4096]{1,0:T(8,128)(2,1)}, bf16[144,4096]{1,0:T(8,128)(2,1)}) custom-call(s32[4]{0:T(128)} %fusion.14.numbers, bf16[128,4096]{1,0:T(8,128)(2,1)} %refs_0_.1, bf16[128,4096]{1,0:T(8,128)(2,1)} %collective-permute-done.3.refs_1_, ...), custom_call_target="tpu_custom_call" | custom-call | flops 1024 | bytes 1024 | tf_op jit(solution)/shard_map/pallas_call | solution.py:257
  81.6 2.0 %collective-permute-start.15 = (bf16[144,4096]{1,0:T(8,128)(2,1)}, bf16[144,4096]{1,0:T(8,128)(2,1)S(1)}, u32[]{:S(2)}, u32[]{:S(2)}) collective-permute-start(bf16[144,4096]{1,0:T(8,128)(2,1)} %get-tuple-element.65), channel_id=1, source_target_pairs={{0,8},{4,28},{8,16},{12,4},{16,24},{20,12},{24,0},{28,20},{1,9},{5... | collective-permute-start | bytes 3538952 | tf_op jit(solution)/shard_map/ppermute | solution.py:35
  83.6 2.2 %collective-permute-start.16 = (bf16[144,4096]{1,0:T(8,128)(2,1)}, bf16[144,4096]{1,0:T(8,128)(2,1)S(1)}, u32[]{:S(2)}, u32[]{:S(2)}) collective-permute-start(bf16[144,4096]{1,0:T(8,128)(2,1)} %get-tuple-element.66), channel_id=1, source_target_pairs={{0,24},{4,12},{8,0},{12,20},{16,8},{20,28},{24,16},{28,4},{1,25},{... | collective-permute-start | bytes 3538952 | tf_op jit(solution)/shard_map/ppermute | solution.py:35
  85.8 3.2 %collective-permute-start.20 = (bf16[528,1024]{1,0:T(8,128)(2,1)}, bf16[528,1024]{1,0:T(8,128)(2,1)}, u32[]{:S(2)}, u32[]{:S(2)}) collective-permute-start(bf16[528,1024]{1,0:T(8,128)(2,1)} %get-tuple-element.72), channel_id=1, source_target_pairs={{0,96},{4,36},{32,0},{36,68},{64,32},{68,100},{96,64},{100,4},{1,9... | collective-permute-start | bytes 3244040 | tf_op jit(solution)/shard_map/ppermute | solution.py:35
  92.8 7.5 %all-to-all-done = bf16[4,128,4096]{2,1,0:T(8,128)(2,1)} async-done(((bf16[4,128,4096]{2,1,0:T(8,128)(2,1)}), bf16[4,128,4096]{2,1,0:T(8,128)(2,1)}, u32[]{:S(2)}, u32[]{:S(2)}) %all-to-all-start) | async-done | bytes 4194336 | tf_op jit(solution)/shard_map/all_to_all | solution.py:320
  100.3 9.5 %collective-permute-done.15 = bf16[144,4096]{1,0:T(8,128)(2,1)S(1)} collective-permute-done((bf16[144,4096]{1,0:T(8,128)(2,1)}, bf16[144,4096]{1,0:T(8,128)(2,1)S(1)}, u32[]{:S(2)}, u32[]{:S(2)}) %collective-permute-start.15) | collective-permute-done | bytes 1179680 | tf_op jit(solution)/shard_map/ppermute | solution.py:35
  109.8 2.5 %collective-permute-done.16 = bf16[144,4096]{1,0:T(8,128)(2,1)S(1)} collective-permute-done((bf16[144,4096]{1,0:T(8,128)(2,1)}, bf16[144,4096]{1,0:T(8,128)(2,1)S(1)}, u32[]{:S(2)}, u32[]{:S(2)}) %collective-permute-start.16) | collective-permute-done | bytes 1179680 | tf_op jit(solution)/shard_map/ppermute | solution.py:35
  114.4 3.2 %convert_reduce_fusion = f32[128,4096]{1,0:T(8,128)S(1)} fusion(bf16[4,128,4096]{2,1,0:T(8,128)(2,1)} %all-to-all-done), kind=kLoop, calls=%fused_computation | loop fusion | flops 3670016 | bytes 6291456 | tf_op jit(solution)/shard_map/reduce_sum | solution.py:331
  119.1 2.2 %add_add_fusion.1 = bf16[512,1024]{1,0:T(8,128)(2,1)S(1)} fusion(bf16[528,1024]{1,0:T(8,128)(2,1)} %collective-permute-done.20, bf16[528,1024]{1,0:T(8,128)(2,1)} %collective-permute-done.19, bf16[528,1024]{1,0:T(8,128)(2,1)S(1)} %copy-done.7), kind=kLoop, calls=%fused_computation.14 | loop fusion | flops 3145728 | bytes 4194304 | tf_op jit(solution)/shard_map/add | solution.py:336
  122.3 9.4 %collective-permute-done.17 = bf16[144,4096]{1,0:T(8,128)(2,1)S(1)} collective-permute-done((bf16[144,4096]{1,0:T(8,128)(2,1)S(1)}, bf16[144,4096]{1,0:T(8,128)(2,1)S(1)}, u32[]{:S(2)}, u32[]{:S(2)}) %collective-permute-start.17) | collective-permute-done | bytes 1179680 | tf_op jit(solution)/shard_map/ppermute | solution.py:35
  132.4 3.3 %collective-permute-start.21 = (bf16[144,1024]{1,0:T(8,128)(2,1)S(1)}, bf16[144,1024]{1,0:T(8,128)(2,1)S(1)}, u32[]{:S(2)}, u32[]{:S(2)}) collective-permute-start(bf16[144,1024]{1,0:T(8,128)(2,1)S(1)} %get-tuple-element.82), channel_id=1, source_target_pairs={{0,2},{4,6},{1,3},{5,7},{2,0},{6,4},{3,1},{7,5},{8,10},{12,14},{9,... | collective-permute-start | bytes 884744 | tf_op jit(solution)/shard_map/ppermute | solution.py:35
  136.2 2.7 %collective-permute-start.23 = (bf16[144,1024]{1,0:T(8,128)(2,1)S(1)}, bf16[144,1024]{1,0:T(8,128)(2,1)S(1)}, u32[]{:S(2)}, u32[]{:S(2)}) collective-permute-start(bf16[144,1024]{1,0:T(8,128)(2,1)S(1)} %get-tuple-element.84), channel_id=1, source_target_pairs={{0,3},{4,5},{1,0},{5,6},{2,1},{6,7},{3,2},{7,4},{8,11},{12,13},{9,... | collective-permute-start | bytes 884744 | tf_op jit(solution)/shard_map/ppermute | solution.py:35
  141.8 2.2 %collective-permute-done.21 = bf16[144,1024]{1,0:T(8,128)(2,1)S(1)} collective-permute-done((bf16[144,1024]{1,0:T(8,128)(2,1)S(1)}, bf16[144,1024]{1,0:T(8,128)(2,1)S(1)}, u32[]{:S(2)}, u32[]{:S(2)}) %collective-permute-start.21) | collective-permute-done | bytes 294944 | tf_op jit(solution)/shard_map/ppermute | solution.py:35
  144.0 2.0 %collective-permute-start.26 = (bf16[144,1024]{1,0:T(8,128)(2,1)S(1)}, bf16[144,1024]{1,0:T(8,128)(2,1)S(1)}, u32[]{:S(2)}, u32[]{:S(2)}) collective-permute-start(bf16[144,1024]{1,0:T(8,128)(2,1)S(1)} %get-tuple-element.80), channel_id=1, source_target_pairs={{0,24},{4,12},{8,0},{12,20},{16,8},{20,28},{24,16},{28,4},{1,25},{... | collective-permute-start | bytes 884744 | tf_op jit(solution)/shard_map/ppermute | solution.py:35
  145.9 2.1 %collective-permute-done.22 = bf16[144,1024]{1,0:T(8,128)(2,1)S(1)} collective-permute-done((bf16[144,1024]{1,0:T(8,128)(2,1)S(1)}, bf16[144,1024]{1,0:T(8,128)(2,1)S(1)}, u32[]{:S(2)}, u32[]{:S(2)}) %collective-permute-start.22) | collective-permute-done | bytes 294944 | tf_op jit(solution)/shard_map/ppermute | solution.py:35
  (94 shorter events, 40.1 us)
Async XLA Ops:
  0.7 21.5 %collective-permute-start.2 = (bf16[128,4096]{1,0:T(8,128)(2,1)}, bf16[128,4096]{1,0:T(8,128)(2,1)}, u32[]{:S(2)}, u32[]{:S(2)}) collective-permute-start(bf16[128,4096]{1,0:T(8,128)(2,1)} %refs_0_.1), channel_id=1, source_target_pairs={{0,32},{4,100},{32,64},{36,4},{64,96},{68,36},{96,0},{100,68},{1,3... | collective-permute-start | bytes 3145736 | tf_op jit(solution)/shard_map/ppermute | solution.py:35
  4.2 26.2 %collective-permute-start = (bf16[544,1024]{1,0:T(8,128)(2,1)S(1)}, bf16[544,1024]{1,0:T(8,128)(2,1)S(1)}, u32[]{:S(2)}, u32[]{:S(2)}) collective-permute-start(bf16[544,1024]{1,0:T(8,128)(2,1)S(1)} %fusion.2.refs_0_), channel_id=1, source_target_pairs={{0,1},{4,7},{1,2},{5,4},{2,3},{6,5},{3,0},{7,6},{8,9},{12,15},{9,1... | collective-permute-start | bytes 3342344 | tf_op jit(solution)/shard_map/ppermute | solution.py:35
  5.7 26.2 %collective-permute-start.1 = (bf16[544,1024]{1,0:T(8,128)(2,1)S(1)}, bf16[544,1024]{1,0:T(8,128)(2,1)}, u32[]{:S(2)}, u32[]{:S(2)}) collective-permute-start(bf16[544,1024]{1,0:T(8,128)(2,1)S(1)} %fusion.2.refs_0_), channel_id=1, source_target_pairs={{0,3},{4,5},{1,0},{5,6},{2,1},{6,7},{3,2},{7,4},{8,11},{12,13},{9,... | collective-permute-start | bytes 3342344 | tf_op jit(solution)/shard_map/ppermute | solution.py:35
  7.5 24.5 %collective-permute-start.4 = (bf16[544,1024]{1,0:T(8,128)(2,1)S(1)}, bf16[544,1024]{1,0:T(8,128)(2,1)}, u32[]{:S(2)}, u32[]{:S(2)}) collective-permute-start(bf16[544,1024]{1,0:T(8,128)(2,1)S(1)} %fusion.2.refs_0_), channel_id=1, source_target_pairs={{0,4},{4,0},{1,5},{5,1},{2,6},{6,2},{3,7},{7,3},{8,12},{12,8},{9,1... | collective-permute-start | bytes 3342344 | tf_op jit(solution)/shard_map/ppermute | solution.py:22
  7.7 18.8 %collective-permute-start.3 = (bf16[128,4096]{1,0:T(8,128)(2,1)S(1)}, bf16[128,4096]{1,0:T(8,128)(2,1)}, u32[]{:S(2)}, u32[]{:S(2)}) collective-permute-start(bf16[128,4096]{1,0:T(8,128)(2,1)S(1)} %copy-done.2), channel_id=1, source_target_pairs={{0,96},{4,36},{32,0},{36,68},{64,32},{68,100},{96,64},{100,4},{1,9... | collective-permute-start | bytes 3145736 | tf_op jit(solution)/shard_map/ppermute | solution.py:35
  32.8 19.5 %collective-permute-start.6 = (bf16[544,1024]{1,0:T(8,128)(2,1)S(1)}, bf16[544,1024]{1,0:T(8,128)(2,1)}, u32[]{:S(2)}, u32[]{:S(2)}) collective-permute-start(bf16[544,1024]{1,0:T(8,128)(2,1)S(1)} %collective-permute-done.refs_3_), channel_id=1, source_target_pairs={{0,1},{4,7},{1,2},{5,4},{2,3},{6,5},{3,0},{7,6},{8,9},{12,15},{9,1... | collective-permute-start | bytes 3342344 | tf_op jit(solution)/shard_map/ppermute | solution.py:35
  33.4 19.0 %collective-permute-start.8 = (bf16[544,1024]{1,0:T(8,128)(2,1)S(1)}, bf16[544,1024]{1,0:T(8,128)(2,1)S(1)}, u32[]{:S(2)}, u32[]{:S(2)}) collective-permute-start(bf16[544,1024]{1,0:T(8,128)(2,1)S(1)} %collective-permute-done.refs_3_), channel_id=1, source_target_pairs={{0,4},{4,0},{1,5},{5,1},{2,6},{6,2},{3,7},{7,3},{8,12},{12,8},{9,1... | collective-permute-start | bytes 3342344 | tf_op jit(solution)/shard_map/ppermute | solution.py:22
  36.0 16.4 %collective-permute-start.9 = (bf16[544,1024]{1,0:T(8,128)(2,1)}, bf16[544,1024]{1,0:T(8,128)(2,1)}, u32[]{:S(2)}, u32[]{:S(2)}) collective-permute-start(bf16[544,1024]{1,0:T(8,128)(2,1)} %collective-permute-done.1.refs_1_), channel_id=1, source_target_pairs={{0,4},{4,0},{1,5},{5,1},{2,6},{6,2},{3,7},{7,3},{8,12},{12,8},{9,1... | collective-permute-start | bytes 3342344 | tf_op jit(solution)/shard_map/ppermute | solution.py:22
  36.0 16.3 %collective-permute-start.7 = (bf16[128,4096]{1,0:T(8,128)(2,1)}, bf16[128,4096]{1,0:T(8,128)(2,1)}, u32[]{:S(2)}, u32[]{:S(2)}) collective-permute-start(bf16[128,4096]{1,0:T(8,128)(2,1)} %collective-permute-done.2.refs_2_), channel_id=1, source_target_pairs={{0,32},{4,100},{32,64},{36,4},{64,96},{68,36},{96,0},{100,68},{1,3... | collective-permute-start | bytes 3145736 | tf_op jit(solution)/shard_map/ppermute | solution.py:35
  36.0 16.3 %collective-permute-start.11 = (bf16[128,4096]{1,0:T(8,128)(2,1)}, bf16[128,4096]{1,0:T(8,128)(2,1)}, u32[]{:S(2)}, u32[]{:S(2)}) collective-permute-start(bf16[128,4096]{1,0:T(8,128)(2,1)} %collective-permute-done.3.refs_1_), channel_id=1, source_target_pairs={{0,4},{4,0},{1,5},{5,1},{2,6},{6,2},{3,7},{7,3},{8,12},{12,8},{9,1... | collective-permute-start | bytes 3145736 | tf_op jit(solution)/shard_map/ppermute | solution.py:22
  46.1 54.2 %all-to-all-start = ((bf16[4,128,4096]{2,1,0:T(8,128)(2,1)}), bf16[4,128,4096]{2,1,0:T(8,128)(2,1)}, u32[]{:S(2)}, u32[]{:S(2)}) async-start(bf16[4,128,4096]{2,1,0:T(8,128)(2,1)} %bitcast.7), calls=%async_computation | async-start | bytes 8388608 | tf_op jit(solution)/shard_map/all_to_all | solution.py:320
  52.5 18.0 %collective-permute-start.12 = (bf16[128,4096]{1,0:T(8,128)(2,1)}, bf16[128,4096]{1,0:T(8,128)(2,1)S(1)}, u32[]{:S(2)}, u32[]{:S(2)}) collective-permute-start(bf16[128,4096]{1,0:T(8,128)(2,1)} %collective-permute-done.7.refs_3_), channel_id=1, source_target_pairs={{0,4},{4,0},{1,5},{5,1},{2,6},{6,2},{3,7},{7,3},{8,12},{12,8},{9,1... | collective-permute-start | bytes 3145736 | tf_op jit(solution)/shard_map/ppermute | solution.py:22
  70.2 18.8 %collective-permute-start.18 = (bf16[528,1024]{1,0:T(8,128)(2,1)}, bf16[528,1024]{1,0:T(8,128)(2,1)}, u32[]{:S(2)}, u32[]{:S(2)}) collective-permute-start(bf16[528,1024]{1,0:T(8,128)(2,1)} %get-tuple-element.71), channel_id=1, source_target_pairs={{0,32},{4,100},{32,64},{36,4},{64,96},{68,36},{96,0},{100,68},{1,3... | collective-permute-start | bytes 3244040 | tf_op jit(solution)/shard_map/ppermute | solution.py:35
  81.6 28.2 %collective-permute-start.15 = (bf16[144,4096]{1,0:T(8,128)(2,1)}, bf16[144,4096]{1,0:T(8,128)(2,1)S(1)}, u32[]{:S(2)}, u32[]{:S(2)}) collective-permute-start(bf16[144,4096]{1,0:T(8,128)(2,1)} %get-tuple-element.65), channel_id=1, source_target_pairs={{0,8},{4,28},{8,16},{12,4},{16,24},{20,12},{24,0},{28,20},{1,9},{5... | collective-permute-start | bytes 3538952 | tf_op jit(solution)/shard_map/ppermute | solution.py:35
  83.6 28.7 %collective-permute-start.16 = (bf16[144,4096]{1,0:T(8,128)(2,1)}, bf16[144,4096]{1,0:T(8,128)(2,1)S(1)}, u32[]{:S(2)}, u32[]{:S(2)}) collective-permute-start(bf16[144,4096]{1,0:T(8,128)(2,1)} %get-tuple-element.66), channel_id=1, source_target_pairs={{0,24},{4,12},{8,0},{12,20},{16,8},{20,28},{24,16},{28,4},{1,25},{... | collective-permute-start | bytes 3538952 | tf_op jit(solution)/shard_map/ppermute | solution.py:35
  85.8 33.3 %collective-permute-start.20 = (bf16[528,1024]{1,0:T(8,128)(2,1)}, bf16[528,1024]{1,0:T(8,128)(2,1)}, u32[]{:S(2)}, u32[]{:S(2)}) collective-permute-start(bf16[528,1024]{1,0:T(8,128)(2,1)} %get-tuple-element.72), channel_id=1, source_target_pairs={{0,96},{4,36},{32,0},{36,68},{64,32},{68,100},{96,64},{100,4},{1,9... | collective-permute-start | bytes 3244040 | tf_op jit(solution)/shard_map/ppermute | solution.py:35
  92.8 26.3 %collective-permute-start.19 = (bf16[528,1024]{1,0:T(8,128)(2,1)}, bf16[528,1024]{1,0:T(8,128)(2,1)}, u32[]{:S(2)}, u32[]{:S(2)}) collective-permute-start(bf16[528,1024]{1,0:T(8,128)(2,1)} %pad_maximum_fusion.1), channel_id=1, source_target_pairs={{0,32},{4,100},{32,64},{36,4},{64,96},{68,36},{96,0},{100,68},{1,3... | collective-permute-start | bytes 3244040 | tf_op jit(solution)/shard_map/ppermute | solution.py:35
  113.9 17.8 %collective-permute-start.17 = (bf16[144,4096]{1,0:T(8,128)(2,1)S(1)}, bf16[144,4096]{1,0:T(8,128)(2,1)S(1)}, u32[]{:S(2)}, u32[]{:S(2)}) collective-permute-start(bf16[144,4096]{1,0:T(8,128)(2,1)S(1)} %pad_maximum_fusion), channel_id=1, source_target_pairs={{0,8},{4,28},{8,16},{12,4},{16,24},{20,12},{24,0},{28,20},{1,9},{5... | collective-permute-start | bytes 3538952 | tf_op jit(solution)/shard_map/ppermute | solution.py:35
  132.4 11.5 %collective-permute-start.21 = (bf16[144,1024]{1,0:T(8,128)(2,1)S(1)}, bf16[144,1024]{1,0:T(8,128)(2,1)S(1)}, u32[]{:S(2)}, u32[]{:S(2)}) collective-permute-start(bf16[144,1024]{1,0:T(8,128)(2,1)S(1)} %get-tuple-element.82), channel_id=1, source_target_pairs={{0,2},{4,6},{1,3},{5,7},{2,0},{6,4},{3,1},{7,5},{8,10},{12,14},{9,... | collective-permute-start | bytes 884744 | tf_op jit(solution)/shard_map/ppermute | solution.py:35
  135.7 12.3 %collective-permute-start.22 = (bf16[144,1024]{1,0:T(8,128)(2,1)S(1)}, bf16[144,1024]{1,0:T(8,128)(2,1)S(1)}, u32[]{:S(2)}, u32[]{:S(2)}) collective-permute-start(bf16[144,1024]{1,0:T(8,128)(2,1)S(1)} %get-tuple-element.83), channel_id=1, source_target_pairs={{0,1},{4,7},{1,2},{5,4},{2,3},{6,5},{3,0},{7,6},{8,9},{12,15},{9,1... | collective-permute-start | bytes 884744 | tf_op jit(solution)/shard_map/ppermute | solution.py:35
  136.2 12.0 %collective-permute-start.23 = (bf16[144,1024]{1,0:T(8,128)(2,1)S(1)}, bf16[144,1024]{1,0:T(8,128)(2,1)S(1)}, u32[]{:S(2)}, u32[]{:S(2)}) collective-permute-start(bf16[144,1024]{1,0:T(8,128)(2,1)S(1)} %get-tuple-element.84), channel_id=1, source_target_pairs={{0,3},{4,5},{1,0},{5,6},{2,1},{6,7},{3,2},{7,4},{8,11},{12,13},{9,... | collective-permute-start | bytes 884744 | tf_op jit(solution)/shard_map/ppermute | solution.py:35
  138.9 13.5 %collective-permute-start.24 = (bf16[144,1024]{1,0:T(8,128)(2,1)S(1)}, bf16[144,1024]{1,0:T(8,128)(2,1)S(1)}, u32[]{:S(2)}, u32[]{:S(2)}) collective-permute-start(bf16[144,1024]{1,0:T(8,128)(2,1)S(1)} %get-tuple-element.78), channel_id=1, source_target_pairs={{0,16},{4,20},{8,24},{12,28},{16,0},{20,4},{24,8},{28,12},{1,17},{... | collective-permute-start | bytes 884744 | tf_op jit(solution)/shard_map/ppermute | solution.py:35
  139.9 14.1 %collective-permute-start.25 = (bf16[144,1024]{1,0:T(8,128)(2,1)S(1)}, bf16[144,1024]{1,0:T(8,128)(2,1)S(1)}, u32[]{:S(2)}, u32[]{:S(2)}) collective-permute-start(bf16[144,1024]{1,0:T(8,128)(2,1)S(1)} %get-tuple-element.79), channel_id=1, source_target_pairs={{0,8},{4,28},{8,16},{12,4},{16,24},{20,12},{24,0},{28,20},{1,9},{5... | collective-permute-start | bytes 884744 | tf_op jit(solution)/shard_map/ppermute | solution.py:35
  144.0 10.1 %collective-permute-start.26 = (bf16[144,1024]{1,0:T(8,128)(2,1)S(1)}, bf16[144,1024]{1,0:T(8,128)(2,1)S(1)}, u32[]{:S(2)}, u32[]{:S(2)}) collective-permute-start(bf16[144,1024]{1,0:T(8,128)(2,1)S(1)} %get-tuple-element.80), channel_id=1, source_target_pairs={{0,24},{4,12},{8,0},{12,20},{16,8},{20,28},{24,16},{28,4},{1,25},{... | collective-permute-start | bytes 884744 | tf_op jit(solution)/shard_map/ppermute | solution.py:35
  (20 other events, 136.7 us)
